TPU v7x, 256 devices: a whole 4x4x8 slice. The times are simulated.
256 devices in a mesh: gy: 32 (over z_hi, y, core), gx: 8 (over x, z_lo).
Axes of the slice: x: 4, y: 4, z: 8 (z_hi: 4, z_lo: 2; z = z_hi * 2 + z_lo), core: 2. Of those that a mesh axis runs over, the one named last changes fastest.
Arguments:
- second_section_map: bfloat16 [1024, 512, 256], P('gy', 'gx'), may hold values from -6 to 6
- convolution_weight: bfloat16 [3, 3, 256, 512], replicated, may hold values from -0.125 to 0.125
- convolution_bias: float32 [512], replicated, may hold values from -3 to 3
- downsampler_gain: float32 [512], replicated, may hold values from 0.25 to 1.75
- downsampler_shift: float32 [512], replicated, may hold values from -2 to 2
- prenorm_gains: float32 [2, 512], replicated, may hold values from 0.25 to 1.75
- prenorm_shifts: float32 [2, 512], replicated, may hold values from -2 to 2
- query_key_value_weight: bfloat16 [2, 512, 1536], replicated, may hold values from -2 to 2
- query_key_value_bias: float32 [2, 1536], replicated, may hold values from -2 to 2
- relative_offset_bias: float32 [2, 16, 49], replicated, may hold values from -4 to 4
- output_projection_weight: bfloat16 [2, 512, 512], replicated, may hold values from -0.25 to 0.25
- output_projection_bias: float32 [2, 512], replicated, may hold values from -2 to 2
Outputs:
- features: bfloat16 [512, 256, 512], P('gy', 'gx')
All inputs are finite; a program needn't handle non-finite values.
Results may differ from a plain program's by a relative error of at most 0.019.
Values may be sent and summed in bfloat16 or wider, within the bound.
No kernel may reach another device: no remote copies, remote signals or barrier semaphores. Data moves between devices by JAX's collectives and lax.ppermute only.
A program may use at most 128 MiB of HBM per device.

v0:
```python
import functools

import jax
import jax.numpy as jnp
import ml_dtypes
import numpy as np
from jax import lax
from jax.experimental import pallas as pl
from jax.experimental.pallas import tpu as pltpu
from jax.sharding import Mesh, PartitionSpec as P

F32 = jnp.float32
BF16 = jnp.bfloat16
KERNEL = 7
HALF = 3
NEG = -1e30
LOG2E = 1.4426950408889634
TR, TC = 16, 32
C2, C3 = 256, 512
HEADS, HD = 16, 32
GROUP = 8
DIL = 8
PAIRS = 11
PT = 80
NTOK = PAIRS * PT
EPS = 1e-5
VMEM_LIMIT = 56 * 1024 * 1024


def pair_slots():
    out = []
    for rp in range(2):
        for c in range(16):
            out.append((rp * 16 + c, rp, c))
        for c in range(16, 22):
            out.append((32 + rp * 6 + c - 16, rp, c))
        for c in range(22, 38):
            out.append((48 + rp * 16 + c - 22, rp, c))
    return out


def pick_matrix():
    pick = np.zeros((3 * PT, 160), np.float32)
    for b in range(3):
        for slot, rp, c in pair_slots():
            col = 2 * c + b - 7
            if col < 0:
                k = 128 + 16 * rp + col + 8
            elif col < 64:
                k = 64 * rp + col
            else:
                k = 128 + 16 * rp + 8 + col - 64
            pick[b * PT + slot, k] = 1
    return pick


def near_keys():
    rows = np.full((2, 256), -99, np.int32)
    cols = np.full((2, 256), -99, np.int32)
    for half in range(2):
        for j in range(5):
            for slot, rp, c in pair_slots():
                at = slot - 32 * half
                if 0 <= at < 48:
                    rows[half, 48 * j + at] = 2 * j + rp
                    cols[half, 48 * j + at] = c - 16 * half
    return rows, cols


def query_matrix():
    rows, cols = near_keys()
    sel = np.zeros((2, 64, 256), np.float32)
    for half in range(2):
        for k in range(256):
            r, c = rows[half, k] - 3, cols[half, k] - 3
            if 0 <= r < 4 and 0 <= c < 16:
                sel[half, r * 16 + c, k] = 1
    return sel


def offset_onehot(qr, qc, kr, kc):
    dr = kr[None, :] - qr[:, None]
    dc = kc[None, :] - qc[:, None]
    near = (np.abs(dr) <= HALF) & (np.abs(dc) <= HALF)
    pos = (dr + HALF) * KERNEL + dc + HALF
    hot = (pos[None] == np.arange(49)[:, None, None]) & near[None]
    return hot.astype(np.float32), near


def near_tables():
    rows, cols = near_keys()
    q = np.arange(64)
    made = [offset_onehot(q // 16 + 3, q % 16 + 3, rows[h], cols[h]) for h in range(2)]
    return np.stack([m[0] for m in made], 1), np.stack([m[1] for m in made])


def far_tables():
    q = np.arange(64)
    k = np.arange(256)
    qr = (q % 8) // 4
    qc = 4 * (q // 8) + q % 4
    return offset_onehot(qr + 3, qc, k // 32, k % 32)


def send_matrix():
    perm = np.zeros((512, 512), np.float32)
    for m in range(4):
        for h in range(2):
            for qr in range(4):
                for qc in range(16):
                    row, col = 4 * m + qr, 16 * h + qc
                    dst = ((row % 8) * 8 + col % 8) * 8 + (row // 8) * 4 + col // 8
                    perm[dst, (m * 2 + h) * 64 + qr * 16 + qc] = 1
    return perm


def far_key_matrix():
    sel = np.zeros((64, 128), np.float32)
    for src in range(2):
        for gx in range(8):
            for a in range(2):
                for b in range(4):
                    if (src == 0) == (a == 1):
                        rp = src
                        sel[rp * 32 + gx * 4 + b, src * 64 + gx * 8 + a * 4 + b] = 1
    return sel


def back_matrix():
    sel = np.zeros((64, 64), np.float32)
    for j in range(8):
        for a in range(2):
            for b in range(4):
                sel[a * 32 + b * 8 + j, j * 8 + a * 4 + b] = 1
    return sel


def bf(x):
    return jnp.asarray(x.astype(ml_dtypes.bfloat16))


def norm(v, gain, shift):
    mean = jnp.mean(v, axis=-1, keepdims=True)
    d = v - mean
    var = jnp.mean(d * d, axis=-1, keepdims=True)
    return d * lax.rsqrt(var + EPS) * gain + shift


def attend_block(q, k, v, table_ref, table_at, extra):
    lane = lax.broadcasted_iota(jnp.int32, (1, 256), 1) // HD
    outs = []
    for g in range(HEADS // GROUP):
        at = slice(256 * g, 256 * g + 256)
        qg, kg, vg = q[:, at], k[:, at], v[:, at]
        stacked = jnp.concatenate(
            [qg * (lane == h).astype(BF16) for h in range(GROUP)], axis=0
        )
        s = lax.dot_general(stacked, kg, (((1,), (1,)), ((), ())), preferred_element_type=F32)
        s = s * (HD**-0.5 * LOG2E) + (table_ref[table_at + (g,)] + extra)
        peak = jnp.max(s, axis=-1, keepdims=True)
        p = jnp.exp2(s - peak)
        total = jnp.sum(p, axis=-1, keepdims=True)
        o = jnp.dot(p.astype(BF16), vg, preferred_element_type=F32) * (1.0 / total)
        acc = jnp.zeros((64, 256), F32)
        for h in range(GROUP):
            acc = jnp.where(lane == h, o[64 * h : 64 * h + 64], acc)
        outs.append(acc)
    return jnp.concatenate(outs, axis=1)


def near_kernel(
    flag_ref, up, own, down, rim, pick, wconv, bconv, gain0, shift0, gain1, shift1, wqkv, bqkv,
    table, extra, qsel, wout, bout, send, out, cat, x0s, ys, ks, vs, yq, xq, qs, att,
):
    flag = flag_ref[0].astype(BF16)

    def main_row(e):
        if e < 7:
            row = up[e]
            return row * flag if e == 6 else row
        return own[e - 7] if e < 39 else down[e - 39]

    def rim_row(e):
        return rim[e] * flag if e == 6 else rim[e]

    for p in range(PAIRS):
        for a in range(3):
            e0, e1 = 4 * p + a, 4 * p + a + 2
            rows = jnp.concatenate([main_row(e0), main_row(e1), rim_row(e0), rim_row(e1)], axis=0)
            got = jnp.dot(pick[...], rows, preferred_element_type=F32).astype(BF16)
            for b in range(3):
                cat[PT * p : PT * p + PT, 256 * (3 * a + b) : 256 * (3 * a + b) + 256] = got[
                    PT * b : PT * b + PT
                ]
    conv = jnp.dot(cat[...], wconv[...], preferred_element_type=F32) + bconv[...]
    x0 = norm(conv, gain0[...], shift0[...]).astype(BF16)
    y = norm(x0.astype(F32), gain1[...], shift1[...]).astype(BF16)
    x0s[...] = x0.reshape(PAIRS, PT, C3)
    ys[...] = y.reshape(PAIRS, PT, C3)
    kv = jnp.dot(y, wqkv[:, C3:], preferred_element_type=F32) + bqkv[:, C3:]
    ks[...] = kv[:, :C3].astype(BF16).reshape(PAIRS, PT, C3)
    vs[...] = kv[:, C3:].astype(BF16).reshape(PAIRS, PT, C3)

    def window(ref, m, h):
        part = ref[pl.ds(2 * m, 5), 32 * h : 32 * h + 48, :].reshape(240, C3)
        return jnp.concatenate([part, part[:16]], axis=0)

    for m in range(4):
        for h in range(2):
            at = slice((2 * m + h) * 64, (2 * m + h) * 64 + 64)
            sel = qsel[h]
            yq[at] = jnp.dot(sel, window(ys, m, h), preferred_element_type=F32).astype(BF16)
            xq[at] = jnp.dot(sel, window(x0s, m, h), preferred_element_type=F32)
    qs[...] = (jnp.dot(yq[...], wqkv[:, :C3], preferred_element_type=F32) + bqkv[:, :C3]).astype(BF16)

    def block(m, _):
        for h in range(2):
            at = pl.ds(pl.multiple_of((2 * m + h) * 64, 64), 64)
            o = attend_block(
                qs[at], window(ks, m, h), window(vs, m, h), table, (h,), extra[pl.ds(2 * m + h, 1), :]
            )
            att[at] = o.astype(BF16)
        return 0

    lax.fori_loop(0, 4, block, 0)
    x1 = jnp.dot(att[...], wout[...], preferred_element_type=F32) + bout[...] + xq[...]
    out[...] = jnp.dot(send[...], x1.astype(BF16), preferred_element_type=F32).astype(BF16)


def far_kernel(
    above, own, below, gain, shift, wqkv, bqkv, ksel, table, extra, wout, bout, out, ys, yk, ks, vs, qs, att
):
    for ref, at, n in ((above, 0, 128), (own, 128, 512), (below, 640, 128)):
        ys[at : at + n] = norm(ref[...].astype(F32), gain[...], shift[...]).astype(BF16)
    for j in range(PAIRS):
        yk[64 * j : 64 * j + 64] = jnp.dot(
            ksel[...], ys[64 * j : 64 * j + 128], preferred_element_type=F32
        ).astype(BF16)
    kv = jnp.dot(yk[...], wqkv[:, C3:], preferred_element_type=F32) + bqkv[:, C3:]
    ks[...] = kv[:, :C3].astype(BF16)
    vs[...] = kv[:, C3:].astype(BF16)
    qs[...] = (
        jnp.dot(ys[128:640], wqkv[:, :C3], preferred_element_type=F32) + bqkv[:, :C3]
    ).astype(BF16)

    def block(m, _):
        at = pl.ds(pl.multiple_of(m * 64, 64), 64)
        keys = pl.ds(pl.multiple_of(m * 64, 64), 256)
        o = attend_block(qs[at], ks[keys], vs[keys], table, (), extra[pl.ds(m, 1), :])
        att[at] = o.astype(BF16)
        return 0

    lax.fori_loop(0, 8, block, 0)
    x2 = jnp.dot(att[...], wout[...], preferred_element_type=F32) + bout[...]
    out[...] = (x2 + own[...].astype(F32)).astype(BF16)


def back_kernel(got, sel, out):
    for i in range(8):
        rows = jnp.dot(sel[...], got[64 * i : 64 * i + 64], preferred_element_type=F32).astype(BF16)
        out[i] = rows[:32]
        out[8 + i] = rows[32:]


def call(kernel, out_shape, scratch, args, smem=0):
    specs = [pl.BlockSpec(memory_space=pltpu.SMEM)] * smem
    specs += [pl.BlockSpec(memory_space=pltpu.VMEM)] * (len(args) - smem)
    return pl.pallas_call(
        kernel,
        out_shape=jax.ShapeDtypeStruct(out_shape, BF16),
        in_specs=specs,
        out_specs=pl.BlockSpec(memory_space=pltpu.VMEM),
        scratch_shapes=[pltpu.VMEM(s, t) for s, t in scratch],
        compiler_params=pltpu.CompilerParams(vmem_limit_bytes=VMEM_LIMIT),
    )(*args)


def per_device(
    zsize, isize, xsize,
    fmap, wconv, bconv, gain0, shift0, gains, shifts, wqkv, bqkv, rel, wout, bout,
):
    zi, ii, xi = lax.axis_index("gz"), lax.axis_index("gi"), lax.axis_index("gx")
    ysize = zsize * isize
    yi = zi * isize + ii

    def shifted(x, dy, dx):
        pairs = [
            (y * xsize + c, ((y + dy) % ysize) * xsize + (c + dx) % xsize)
            for y in range(ysize)
            for c in range(xsize)
        ]
        return lax.ppermute(x, ("gz", "gi", "gx"), pairs)

    up = shifted(fmap[25:], 1, 0)
    down = shifted(fmap[:6], -1, 0)

    def tables(hot, near, layer):
        t = jnp.einsum("ho,o...->h...", rel[layer], jnp.asarray(hot), precision=lax.Precision.HIGHEST)
        return jnp.where(jnp.asarray(near)[None], t * LOG2E, NEG)

    hot0, near0 = near_tables()
    table0 = tables(hot0, near0, 0).transpose(1, 0, 2, 3).reshape(2, 2, GROUP * 64, 256)
    hot1, near1 = far_tables()
    table1 = tables(hot1, near1, 1).reshape(2, GROUP * 64, 256)

    krow, kcol = near_keys()
    rows0 = yi * TR - 3 + np.repeat(np.arange(4) * 4, 2)[:, None] + np.tile(krow, (4, 1))
    cols0 = xi * TC - 3 + np.tile(np.arange(2) * 16, 4)[:, None] + np.tile(kcol, (4, 1))
    inside0 = (rows0 >= 0) & (rows0 < ysize * TR) & (cols0 >= 0) & (cols0 < xsize * TC)
    extra0 = jnp.where(inside0, 0.0, NEG).astype(F32)
    rows1 = zi * 16 - 3 + 2 * np.arange(8)[:, None] + np.arange(256)[None] // 32
    extra1 = jnp.where((rows1 >= 0) & (rows1 < zsize * 16), 0.0, NEG).astype(F32)

    def strip(at):
        return jnp.concatenate([up[:, at], fmap[:, at], down[:, at]], axis=0)

    left = shifted(strip(slice(56, 64)), 0, 1)
    right = shifted(strip(slice(0, 8)), 0, -1)
    rim = jnp.concatenate([jnp.where(xi == 0, jnp.zeros_like(left), left), right], axis=1)
    flag = jnp.where(yi == 0, 0.0, 1.0).astype(F32).reshape(1)

    row = lambda v: v.reshape(1, -1)
    x1 = call(
        near_kernel,
        (512, C3),
        [
            ((NTOK, 9 * C2), BF16), ((PAIRS, PT, C3), BF16), ((PAIRS, PT, C3), BF16),
            ((PAIRS, PT, C3), BF16), ((PAIRS, PT, C3), BF16), ((512, C3), BF16), ((512, C3), F32),
            ((512, C3), BF16), ((512, C3), BF16),
        ],
        [
            flag, up, fmap, down, rim, bf(pick_matrix()), wconv.reshape(9 * C2, C3), row(bconv),
            row(gain0), row(shift0), row(gains[0]), row(shifts[0]), wqkv[0], row(bqkv[0]), table0,
            extra0, bf(query_matrix()), wout[0], row(bout[0]), bf(send_matrix()),
        ],
        smem=1,
    )
    got = lax.all_to_all(x1.reshape(64, 8, C3), ("gi", "gx"), 0, 0).reshape(512, C3)
    step = isize
    above = shifted(got[384:], step, 0)
    below = shifted(got[:128], -step, 0)
    x2 = call(
        far_kernel,
        (512, C3),
        [
            ((768, C3), BF16), ((704, C3), BF16), ((704, C3), BF16), ((704, C3), BF16),
            ((512, C3), BF16), ((512, C3), BF16),
        ],
        [
            above, got, below, row(gains[1]), row(shifts[1]), wqkv[1], row(bqkv[1]),
            bf(far_key_matrix()), table1, extra1, wout[1], row(bout[1]),
        ],
    )
    back = lax.all_to_all(x2.reshape(64, 8, C3), ("gi", "gx"), 0, 0).reshape(512, C3)
    return call(back_kernel, (TR, TC, C3), [], [back, bf(back_matrix())])


def solution(mesh):
    gy, gx = mesh.shape["gy"], mesh.shape["gx"]
    inner = Mesh(mesh.devices.reshape(gy // 8, 8, gx), ("gz", "gi", "gx"))
    tile = P(("gz", "gi"), "gx", None)
    placed = (tile,) + (P(),) * 11
    return jax.shard_map(
        functools.partial(per_device, gy // 8, 8, gx),
        mesh=inner,
        in_specs=placed,
        out_specs=tile,
        check_vma=False,
    )
```

profile of v0, /device:TPU:1, one launch (start us, length us, event | category | flops | bytes accessed | tf_op | source)
XLA Modules:
  0.0 118.1 jit_solution(16595919483557191603)
XLA Ops:
  0.0 1.0 slice.78
  1.0 2.8 %collective-permute-start = (bf16[7,64,256]{2,1,0:T(8,128)(2,1)S(1)}, bf16[7,64,256]{2,1,0:T(8,128)(2,1)S(1)}, u32[]{:S(2)}, u32[]{:S(2)}) collective-permute-start(bf16[7,64,256]{2,1,0:T(8,128)(2,1)S(1)} %slice.78), channel_id=1, source_target_pairs={{0,8},{1,9},{2,10},{3,11},{4,12},{5,13},{6,14},{7,15},{8,16},{9,17... | collective-permute-start | bytes 688136 | tf_op jit(solution)/shard_map/ppermute | solution.py:292
  3.7 0.9 slice.79
  4.7 0.6 collective-permute-start.1
  5.3 1.0 fusion.8
  6.3 0.0 copy-start.6
  6.4 3.9 %slice_bitcast_fusion = (bf16[512,1536]{1,0:T(8,128)(2,1)}, bf16[512,1536]{1,0:T(8,128)(2,1)}) fusion(bf16[2,512,1536]{2,1,0:T(8,128)(2,1)} %param.34), kind=kLoop, calls=%fused_computation.1 | loop fusion | bytes 6291456 | tf_op jit(solution)/shard_map/squeeze | solution.py:350
  10.2 0.6 fusion.11
  10.9 1.0 slice_bitcast_fusion.2
  12.0 7.1 %select_bitcast_fusion = f32[2,16,64,256]{3,1,2,0:T(8,128)S(1)} fusion(f32[49,2,64,256]{3,0,2,1:T(8,128)} %constant.73.clone, pred[2,64,256]{2,1,0:T(8,128)(4,1)S(1)} %copy.31, f32[2,16,49]{2,1,0:T(8,128)S(1)} %copy-done.8), kind=kOutput, calls=%fused_computation | convolution fusion | flops 309329920 | bytes 8560640 | tf_op jit(solution)/shard_map/ho,o...->h.../dot_general | solution.py:298
  19.1 0.7 fusion.5.extra
  19.8 0.6 fusion.12
  20.5 1.2 collective-permute-start.2
  21.7 0.6 fusion.14
  22.2 2.6 %copy.28 = f32[2,16,64,256]{3,2,1,0:T(8,128)} copy(f32[2,16,64,256]{3,1,2,0:T(8,128)S(1)} %select_bitcast_fusion) | data formatting | bytes 4194304 | tf_op jit(solution)/shard_map/jit(_where)/select_n | solution.py:299
  24.8 2.7 %collective-permute-start.3 = (bf16[45,8,256]{2,1,0:T(8,128)(2,1)S(1)}, bf16[45,8,256]{2,1,0:T(8,128)(2,1)S(1)}, u32[]{:S(2)}, u32[]{:S(2)}) collective-permute-start(bf16[45,8,256]{2,1,0:T(8,128)(2,1)S(1)} %pad_maximum_fusion.2), channel_id=1, source_target_pairs={{0,7},{1,0},{2,1},{3,2},{4,3},{5,4},{6,5},{7,6},{8,15},{9,8},{10,9... | collective-permute-start | bytes 552968 | tf_op jit(solution)/shard_map/ppermute | solution.py:292
  27.6 3.9 %collective-permute-done.3 = bf16[45,8,256]{2,1,0:T(8,128)(2,1)S(1)} collective-permute-done((bf16[45,8,256]{2,1,0:T(8,128)(2,1)S(1)}, bf16[45,8,256]{2,1,0:T(8,128)(2,1)S(1)}, u32[]{:S(2)}, u32[]{:S(2)}) %collective-permute-start.3) | collective-permute-done | bytes 184352 | tf_op jit(solution)/shard_map/ppermute | solution.py:292
  31.5 0.8 pad_maximum_fusion.rim
  32.2 16.2 %shard_map.253 = bf16[512,512]{1,0:T(8,128)(2,1)} custom-call(f32[1]{0:T(128)} %bitcast.flag_ref, bf16[7,64,256]{2,1,0:T(8,128)(2,1)} %copy-done.2, bf16[32,64,256]{2,1,0:T(8,128)(2,1)} %own.1, bf16[6,64,256]{2,1,0:T(8,128)(2,1)} %copy-done.3, bf16[45,16,256]{2,1,0:T(8,128)(2,1)} %pad_maximum_fusion.rim, bf16[240,160]{1,0:T(8,128)(2,1)} %constant.83.clone.pick, ...), custom_call_target="tpu_custom_call" | custom-call | tf_op jit(solution)/shard_map/pallas_call | solution.py:268
  48.4 12.6 %all-to-all-start = ((bf16[64,8,512]{2,1,0:T(8,128)(2,1)}), bf16[64,8,512]{2,1,0:T(8,128)(2,1)S(1)}, u32[]{:S(2)}, u32[]{:S(2)}) async-start(bf16[64,8,512]{2,1,0:T(8,128)(2,1)} %bitcast.50), calls=%async_computation | async-start | bytes 1048576 | tf_op jit(solution)/shard_map/all_to_all | solution.py:338
  61.1 4.6 %fusion.1 = f32[16,64,256]{2,0,1:T(8,128)S(1)} fusion(f32[49,64,256]{2,0,1:T(8,128)} %constant.75.clone, pred[64,256]{1,0:T(8,128)(4,1)S(1)} %copy.32, f32[2,16,49]{2,1,0:T(8,128)S(1)} %copy-done.8), kind=kOutput, calls=%fused_computation.5 | convolution fusion | flops 154664960 | bytes 4284416 | tf_op jit(solution)/shard_map/ho,o...->h.../dot_general | solution.py:298
  65.7 1.6 %copy.29 = f32[16,64,256]{2,1,0:T(8,128)} copy(f32[16,64,256]{2,0,1:T(8,128)S(1)} %fusion.1) | data formatting | bytes 2097152 | tf_op jit(solution)/shard_map/jit(_where)/select_n | solution.py:299
  67.3 6.2 %all-to-all-done = bf16[64,8,512]{2,1,0:T(8,128)(2,1)S(1)} async-done(((bf16[64,8,512]{2,1,0:T(8,128)(2,1)}), bf16[64,8,512]{2,1,0:T(8,128)(2,1)S(1)}, u32[]{:S(2)}, u32[]{:S(2)}) %all-to-all-start) | async-done | bytes 524320 | tf_op jit(solution)/shard_map/all_to_all | solution.py:338
  73.5 0.5 collective-permute-start.4
  74.0 3.2 %collective-permute-start.5 = (bf16[128,512]{1,0:T(8,128)(2,1)S(1)}, bf16[128,512]{1,0:T(8,128)(2,1)S(1)}, u32[]{:S(2)}, u32[]{:S(2)}) collective-permute-start(bf16[128,512]{1,0:T(8,128)(2,1)S(1)} %get-tuple-element.11), channel_id=1, source_target_pairs={{0,192},{1,193},{2,194},{3,195},{4,196},{5,197},{6,198},{7,199},{8... | collective-permute-start | bytes 393224 | tf_op jit(solution)/shard_map/ppermute | solution.py:292
  77.2 0.7 fusion.7.extra
  77.9 6.1 %collective-permute-done.4.above = bf16[128,512]{1,0:T(8,128)(2,1)S(1)} collective-permute-done((bf16[128,512]{1,0:T(8,128)(2,1)S(1)}, bf16[128,512]{1,0:T(8,128)(2,1)S(1)}, u32[]{:S(2)}, u32[]{:S(2)}) %collective-permute-start.4) | collective-permute-done | bytes 131104 | tf_op jit(solution)/shard_map/ppermute | solution.py:292
  84.0 1.2 %collective-permute-done.5.below = bf16[128,512]{1,0:T(8,128)(2,1)S(1)} collective-permute-done((bf16[128,512]{1,0:T(8,128)(2,1)S(1)}, bf16[128,512]{1,0:T(8,128)(2,1)S(1)}, u32[]{:S(2)}, u32[]{:S(2)}) %collective-permute-start.5) | collective-permute-done | bytes 131104 | tf_op jit(solution)/shard_map/ppermute | solution.py:292
  85.2 0.6 copy-done.5
  85.8 12.3 %shard_map.254 = bf16[512,512]{1,0:T(8,128)(2,1)} custom-call(bf16[128,512]{1,0:T(8,128)(2,1)} %copy-done.4, bf16[512,512]{1,0:T(8,128)(2,1)} %bitcast.48, bf16[128,512]{1,0:T(8,128)(2,1)} %copy-done.5, f32[1,512]{1,0:T(1,128)} %get-tuple-element.23.gain, f32[1,512]{1,0:T(1,128)} %get-tuple-element.28.shift, bf16[512,1536]{1,0:T(8,128)(2,1)} %get-tuple-element.5.wqkv, ...), custom_call_target="tpu_custom_call" | custom-call | tf_op jit(solution)/shard_map/pallas_call | solution.py:268
  98.1 17.9 %all_to_all.10 = bf16[64,8,512]{2,1,0:T(8,128)(2,1)} all-to-all(bf16[64,8,512]{2,1,0:T(8,128)(2,1)} %bitcast.51), channel_id=1, replica_groups=mesh['gz'=4,'gi'=8,'gx'=8] {'gi','gx'}, dimensions={0} | all-to-all | bytes 1048576 | tf_op jit(solution)/shard_map/all_to_all | solution.py:354
  116.0 2.1 %shard_map.255 = bf16[16,32,512]{2,1,0:T(8,128)(2,1)} custom-call(bf16[512,512]{1,0:T(8,128)(2,1)} %bitcast.52, bf16[64,64]{1,0:T(8,128)(2,1)} %constant.87.clone.sel), custom_call_target="tpu_custom_call" | custom-call | tf_op jit(solution)/shard_map/pallas_call | solution.py:268
  (49 shorter events, 0.2 us)
Async XLA Ops:
  1.0 19.5 %collective-permute-start = (bf16[7,64,256]{2,1,0:T(8,128)(2,1)S(1)}, bf16[7,64,256]{2,1,0:T(8,128)(2,1)S(1)}, u32[]{:S(2)}, u32[]{:S(2)}) collective-permute-start(bf16[7,64,256]{2,1,0:T(8,128)(2,1)S(1)} %slice.78), channel_id=1, source_target_pairs={{0,8},{1,9},{2,10},{3,11},{4,12},{5,13},{6,14},{7,15},{8,16},{9,17... | collective-permute-start | bytes 688136 | tf_op jit(solution)/shard_map/ppermute | solution.py:292
  4.7 15.7 %collective-permute-start.1 = (bf16[6,64,256]{2,1,0:T(8,128)(2,1)S(1)}, bf16[6,64,256]{2,1,0:T(8,128)(2,1)S(1)}, u32[]{:S(2)}, u32[]{:S(2)}) collective-permute-start(bf16[6,64,256]{2,1,0:T(8,128)(2,1)S(1)} %slice.79), channel_id=1, source_target_pairs={{0,248},{1,249},{2,250},{3,251},{4,252},{5,253},{6,254},{7,255},{8... | collective-permute-start | bytes 589832 | tf_op jit(solution)/shard_map/ppermute | solution.py:292
  6.3 3.9 %copy-start.9 = (f32[2,1536]{1,0:T(2,128)S(1)}, f32[2,1536]{1,0:T(2,128)}, u32[]{:S(2)}) copy-start(f32[2,1536]{1,0:T(2,128)} %param.35) | copy-start | bytes 36868
  6.3 4.5 %copy-start.6 = (pred[2,64,256]{2,1,0:T(32,128)(4,1)S(1)}, pred[2,64,256]{2,1,0:T(32,128)(4,1)}, u32[]{:S(2)}) copy-start(pred[2,64,256]{2,1,0:T(32,128)(4,1)} %constant.74.clone) | copy-start | bytes 98308
  6.3 4.6 %copy-start.1 = (bf16[2,512,512]{2,1,0:T(8,128)(2,1)S(1)}, bf16[2,512,512]{2,1,0:T(8,128)(2,1)}, u32[]{:S(2)}) copy-start(bf16[2,512,512]{2,1,0:T(8,128)(2,1)} %param.37) | copy-start | bytes 3145732
  6.3 5.6 %copy-start.8 = (f32[2,16,49]{2,1,0:T(8,128)S(1)}, f32[2,16,49]{2,1,0:T(8,128)}, u32[]{:S(2)}) copy-start(f32[2,16,49]{2,1,0:T(8,128)} %param.36) | copy-start | bytes 18820
  11.9 7.1 %copy-start.16 = (s32[8,1]{0,1:T(1,128)S(1)}, s32[8,1]{0,1:T(1,128)}, u32[]{:S(2)}) copy-start(s32[8,1]{0,1:T(1,128)} %constant.79.clone) | copy-start | bytes 100
  11.9 7.1 %copy-start.17 = (s32[8,1]{0,1:T(1,128)S(1)}, s32[8,1]{0,1:T(1,128)}, u32[]{:S(2)}) copy-start(s32[8,1]{0,1:T(1,128)} %constant.77.clone) | copy-start | bytes 100
  11.9 7.2 %copy-start.10 = (s32[8,256]{1,0:T(8,128)S(1)}, s32[8,256]{1,0:T(8,128)}, u32[]{:S(2)}) copy-start(s32[8,256]{1,0:T(8,128)} %constant.78.clone) | copy-start | bytes 24580
  12.0 7.2 %copy-start.11 = (s32[8,256]{1,0:T(8,128)S(1)}, s32[8,256]{1,0:T(8,128)}, u32[]{:S(2)}) copy-start(s32[8,256]{1,0:T(8,128)} %constant.80.clone) | copy-start | bytes 24580
  12.0 7.8 %copy-start.13 = (f32[2,512]{1,0:T(2,128)S(1)}, f32[2,512]{1,0:T(2,128)}, u32[]{:S(2)}) copy-start(f32[2,512]{1,0:T(2,128)} %param.38) | copy-start | bytes 12292
  12.0 7.8 %copy-start.14 = (f32[2,512]{1,0:T(2,128)S(1)}, f32[2,512]{1,0:T(2,128)}, u32[]{:S(2)}) copy-start(f32[2,512]{1,0:T(2,128)} %param.33) | copy-start | bytes 12292
  12.0 9.7 %copy-start.12 = (f32[2,512]{1,0:T(2,128)S(1)}, f32[2,512]{1,0:T(2,128)}, u32[]{:S(2)}) copy-start(f32[2,512]{1,0:T(2,128)} %param.32) | copy-start | bytes 12292
  20.4 4.4 %copy-start.3 = (bf16[6,64,256]{2,1,0:T(8,128)(2,1)}, bf16[6,64,256]{2,1,0:T(8,128)(2,1)S(1)}, u32[]{:S(2)}) copy-start(bf16[6,64,256]{2,1,0:T(8,128)(2,1)S(1)} %collective-permute-done.1.down) | copy-start | bytes 589828
  20.4 4.4 %copy-start.2 = (bf16[7,64,256]{2,1,0:T(8,128)(2,1)}, bf16[7,64,256]{2,1,0:T(8,128)(2,1)S(1)}, u32[]{:S(2)}) copy-start(bf16[7,64,256]{2,1,0:T(8,128)(2,1)S(1)} %collective-permute-done.up) | copy-start | bytes 688132
  20.5 7.1 %collective-permute-start.2 = (bf16[45,8,256]{2,1,0:T(8,128)(2,1)S(1)}, bf16[45,8,256]{2,1,0:T(8,128)(2,1)S(1)}, u32[]{:S(2)}, u32[]{:S(2)}) collective-permute-start(bf16[45,8,256]{2,1,0:T(8,128)(2,1)S(1)} %pad_maximum_fusion.1), channel_id=1, source_target_pairs={{0,1},{1,2},{2,3},{3,4},{4,5},{5,6},{6,7},{7,0},{8,9},{9,10},{10,1... | collective-permute-start | bytes 552968 | tf_op jit(solution)/shard_map/ppermute | solution.py:292
  24.8 6.6 %collective-permute-start.3 = (bf16[45,8,256]{2,1,0:T(8,128)(2,1)S(1)}, bf16[45,8,256]{2,1,0:T(8,128)(2,1)S(1)}, u32[]{:S(2)}, u32[]{:S(2)}) collective-permute-start(bf16[45,8,256]{2,1,0:T(8,128)(2,1)S(1)} %pad_maximum_fusion.2), channel_id=1, source_target_pairs={{0,7},{1,0},{2,1},{3,2},{4,3},{5,4},{6,5},{7,6},{8,15},{9,8},{10,9... | collective-permute-start | bytes 552968 | tf_op jit(solution)/shard_map/ppermute | solution.py:292
  32.2 28.8 %copy-start.7 = (pred[64,256]{1,0:T(32,128)(4,1)S(1)}, pred[64,256]{1,0:T(32,128)(4,1)}, u32[]{:S(2)}) copy-start(pred[64,256]{1,0:T(32,128)(4,1)} %constant.76.clone) | copy-start | bytes 49156
  48.4 25.1 %all-to-all-start = ((bf16[64,8,512]{2,1,0:T(8,128)(2,1)}), bf16[64,8,512]{2,1,0:T(8,128)(2,1)S(1)}, u32[]{:S(2)}, u32[]{:S(2)}) async-start(bf16[64,8,512]{2,1,0:T(8,128)(2,1)} %bitcast.50), calls=%async_computation | async-start | bytes 1048576 | tf_op jit(solution)/shard_map/all_to_all | solution.py:338
  61.1 6.2 %copy-start.18 = (s32[8,1]{0,1:T(1,128)S(1)}, s32[8,1]{0,1:T(1,128)}, u32[]{:S(2)}) copy-start(s32[8,1]{0,1:T(1,128)} %constant.81.clone) | copy-start | bytes 100
  65.7 11.5 %copy-start.15 = (s32[256]{0:T(256)S(1)}, s32[256]{0:T(256)}, u32[]{:S(2)}) copy-start(s32[256]{0:T(256)} %constant.88) | copy-start | bytes 3076
  73.5 11.6 %copy-start = (bf16[64,8,512]{2,1,0:T(8,128)(2,1)}, bf16[64,8,512]{2,1,0:T(8,128)(2,1)S(1)}, u32[]{:S(2)}) copy-start(bf16[64,8,512]{2,1,0:T(8,128)(2,1)S(1)} %all-to-all-done) | copy-start | bytes 1572868
  73.5 10.4 %collective-permute-start.4 = (bf16[128,512]{1,0:T(8,128)(2,1)S(1)}, bf16[128,512]{1,0:T(8,128)(2,1)S(1)}, u32[]{:S(2)}, u32[]{:S(2)}) collective-permute-start(bf16[128,512]{1,0:T(8,128)(2,1)S(1)} %get-tuple-element.12), channel_id=1, source_target_pairs={{0,64},{1,65},{2,66},{3,67},{4,68},{5,69},{6,70},{7,71},{8,72},{9,... | collective-permute-start | bytes 393224 | tf_op jit(solution)/shard_map/ppermute | solution.py:292
  74.0 11.2 %collective-permute-start.5 = (bf16[128,512]{1,0:T(8,128)(2,1)S(1)}, bf16[128,512]{1,0:T(8,128)(2,1)S(1)}, u32[]{:S(2)}, u32[]{:S(2)}) collective-permute-start(bf16[128,512]{1,0:T(8,128)(2,1)S(1)} %get-tuple-element.11), channel_id=1, source_target_pairs={{0,192},{1,193},{2,194},{3,195},{4,196},{5,197},{6,198},{7,199},{8... | collective-permute-start | bytes 393224 | tf_op jit(solution)/shard_map/ppermute | solution.py:292
  84.0 1.2 %copy-start.4 = (bf16[128,512]{1,0:T(8,128)(2,1)}, bf16[128,512]{1,0:T(8,128)(2,1)S(1)}, u32[]{:S(2)}) copy-start(bf16[128,512]{1,0:T(8,128)(2,1)S(1)} %collective-permute-done.4.above) | copy-start | bytes 393220
  85.2 0.7 copy-start.5
where the time goes:
time: 118 us
  Pallas kernels  30.5 us (26%)
  starting transfers between devices  23.6 us (20%)
  blocking collectives  17.9 us (15%)
  waiting for transfers between devices  17.4 us (15%)
  local copies, waits for them, and re-layouts  14.5 us (12%)
  matrix products  11.6 us (10%)
  other arithmetic  2.2 us (2%)
    pallas_call x3, Pallas kernels, call(): pl.pallas_call(kernel, out_shape=jax.ShapeDtypeStruct(out_shape, BF16), i...  30.5 us
    all_to_all x1, blocking collectives, per_device(): lax.all_to_all(x2.reshape(64, 8, C3), ('gi', 'gx'), 0, 0).reshape(512, C3)  17.9 us
    all_to_all x1, starting transfers between devices, per_device(): lax.all_to_all(x1.reshape(64, 8, C3), ('gi', 'gx'), 0, 0).reshape(512, C3)  12.6 us
    dot_general x2, matrix products, tables(): jnp.einsum('ho,o...->h...', rel[layer], jnp.asarray(hot), precision=lax.P...  11.6 us
    ppermute x6, waiting for transfers between devices, shifted(): return lax.ppermute(x, ('gz', 'gi', 'gx'), pairs)  11.2 us
    ppermute x6, starting transfers between devices, shifted(): return lax.ppermute(x, ('gz', 'gi', 'gx'), pairs)  11 us
    all_to_all x1, waiting for transfers between devices, per_device(): lax.all_to_all(x1.reshape(64, 8, C3), ('gi', 'gx'), 0, 0).reshape(512, C3)  6.24 us
    select_n x2, local copies, waits for them, and re-layouts, tables(): return jnp.where(jnp.asarray(near)[None], t * LOG2E, NEG)  4.15 us
  transfers between devices with their start and end apart: 7, of which 4 were waited for; matrix products, arithmetic and copies ran while one was open for 22% of the time, Pallas kernels for 0%

commit v1 on v0

v1 whole, which is shorter than its diff:
```python
import functools

import jax
import jax.numpy as jnp
import ml_dtypes
import numpy as np
from jax import lax
from jax.experimental import pallas as pl
from jax.experimental.pallas import tpu as pltpu
from jax.sharding import Mesh, PartitionSpec as P

F32 = jnp.float32
BF16 = jnp.bfloat16
KERNEL = 7
HALF = 3
NEG = -1e30
LOG2E = 1.4426950408889634
TR, TC = 16, 32
C2, C3 = 256, 512
HEADS, HD = 16, 32
GROUP = 8
DIL = 8
PAIRS = 11
PT = 80
NTOK = PAIRS * PT
EPS = 1e-5
VMEM_LIMIT = 36 * 1024 * 1024


def pair_slots():
    out = []
    for rp in range(2):
        for c in range(16):
            out.append((rp * 16 + c, rp, c))
        for c in range(16, 22):
            out.append((32 + rp * 8 + c - 16, rp, c))
        for c in range(22, 38):
            out.append((48 + rp * 16 + c - 22, rp, c))
    return out


def pick_matrix():
    pick = np.zeros((3 * PT, 160), np.float32)
    for b in range(3):
        for slot, rp, c in pair_slots():
            col = 2 * c + b - 7
            if col < 0:
                k = 128 + 8 * rp + col + 8
            elif col < 64:
                k = 64 * rp + col
            else:
                k = 144 + 8 * rp + col - 64
            pick[b * PT + slot, k] = 1
    return pick


def near_keys():
    rows = np.full((2, 256), -99, np.int32)
    cols = np.full((2, 256), -99, np.int32)
    for half in range(2):
        for j in range(5):
            for slot, rp, c in pair_slots():
                at = slot - 32 * half
                if 0 <= at < 48:
                    rows[half, 48 * j + at] = 2 * j + rp
                    cols[half, 48 * j + at] = c - 16 * half
    return rows, cols


def query_matrix():
    rows, cols = near_keys()
    sel = np.zeros((2, 64, 256), np.float32)
    for half in range(2):
        for k in range(256):
            r, c = rows[half, k] - 3, cols[half, k] - 3
            if 0 <= r < 4 and 0 <= c < 16:
                sel[half, r * 16 + c, k] = 1
    return sel


def near_patterns():
    rows, cols = near_keys()
    hot = np.zeros((49, 2, 2, 4, 256), np.float32)
    code = np.zeros((2, 64, 256), np.int32)
    for half in range(2):
        for k in range(256):
            if rows[half, k] < 0:
                continue
            wide = (cols[half, k] < 16) if half == 0 else (cols[half, k] >= 6)
            for q in range(64):
                dr, dc = rows[half, k] - q // 16, cols[half, k] - q % 16
                if 0 <= dr < 7 and 0 <= dc < 7:
                    part = 0 if wide else 1
                    code[half, q, k] = 1 + part
                    hot[dr * 7 + dc, half, part, q // 16, (k - q % 16) % 256] = 1
    return hot.reshape(49, 4096), code


def far_patterns():
    hot = np.zeros((49, 2, 256), np.float32)
    code = np.zeros((64, 256), np.int32)
    for q in range(64):
        gx, a, b = q // 8, q % 8 // 4, q % 4
        for k in range(256):
            dr, dc = k // 32 - a, k % 32 - (4 * gx + b) + 3
            if 0 <= dr < 7 and 0 <= dc < 7:
                code[q, k] = 1
                hot[dr * 7 + dc, a, (k - 4 * gx - 4 * a - b) % 256] = 1
    return hot.reshape(49, 512), code


def send_matrix():
    perm = np.zeros((512, 512), np.float32)
    for m in range(4):
        for h in range(2):
            for qr in range(4):
                for qc in range(16):
                    row, col = 4 * m + qr, 16 * h + qc
                    dst = ((row % 8) * 8 + col % 8) * 8 + (row // 8) * 4 + col // 8
                    perm[dst, (m * 2 + h) * 64 + qr * 16 + qc] = 1
    return perm


def far_key_matrix():
    sel = np.zeros((64, 128), np.float32)
    for src in range(2):
        for gx in range(8):
            for a in range(2):
                for b in range(4):
                    if (src == 0) == (a == 1):
                        rp = src
                        sel[rp * 32 + gx * 4 + b, src * 64 + gx * 8 + a * 4 + b] = 1
    return sel


def back_matrix():
    sel = np.zeros((64, 64), np.float32)
    for j in range(8):
        for a in range(2):
            for b in range(4):
                sel[a * 32 + b * 8 + j, j * 8 + a * 4 + b] = 1
    return sel


def bf(x):
    return jnp.asarray(x.astype(ml_dtypes.bfloat16))


def norm(v, gain, shift):
    mean = jnp.mean(v, axis=-1, keepdims=True)
    d = v - mean
    var = jnp.mean(d * d, axis=-1, keepdims=True)
    return d * lax.rsqrt(var + EPS) * gain + shift


def attend_block(q, k, v, table, extra):
    lane = lax.broadcasted_iota(jnp.int32, (1, 256), 1) // HD
    outs = []
    for g in range(HEADS // GROUP):
        at = slice(256 * g, 256 * g + 256)
        qg, kg, vg = q[:, at], k[:, at], v[:, at]
        stacked = jnp.concatenate(
            [qg * (lane == h).astype(BF16) for h in range(GROUP)], axis=0
        )
        s = lax.dot_general(stacked, kg, (((1,), (1,)), ((), ())), preferred_element_type=F32)
        s = s * (HD**-0.5 * LOG2E) + (table(g) + extra)
        peak = jnp.max(s, axis=-1, keepdims=True)
        p = jnp.exp2(s - peak)
        total = jnp.sum(p, axis=-1, keepdims=True)
        o = jnp.dot(p.astype(BF16), vg, preferred_element_type=F32) * (1.0 / total)
        acc = jnp.zeros((64, 256), F32)
        for h in range(GROUP):
            acc = jnp.where(lane == h, o[64 * h : 64 * h + 64], acc)
        outs.append(acc)
    return jnp.concatenate(outs, axis=1)


def table_kernel(rel, hot0, code0, hot1, code1, t0, t1):
    def spread(r, hot):
        hi = r.astype(BF16)
        mid = (r - hi.astype(F32)).astype(BF16)
        lo = (r - hi.astype(F32) - mid.astype(F32)).astype(BF16)
        dot = functools.partial(jnp.dot, preferred_element_type=F32)
        return (dot(hi, hot[...]) + dot(mid, hot[...]) + dot(lo, hot[...])) * LOG2E

    e0 = spread(rel[0], hot0)
    e1 = spread(rel[1], hot1)
    for h in range(HEADS):
        for half in range(2):
            for qr in range(4):
                part = []
                for i in range(2):
                    at = ((half * 2 + i) * 4 + qr) * 256
                    one = jnp.broadcast_to(e0[h : h + 1, at : at + 256], (16, 256))
                    part.append(pltpu.roll(one, 0, 1, stride=1, stride_axis=0))
                code = code0[half, 16 * qr : 16 * qr + 16]
                row = h % GROUP * 64 + 16 * qr
                t0[half, h // GROUP, row : row + 16] = jnp.where(
                    code == 1, part[0], jnp.where(code == 2, part[1], NEG)
                )
        two = jnp.concatenate(
            [jnp.broadcast_to(e1[h : h + 1, 256 * a : 256 * a + 256], (4, 256)) for a in range(2)], axis=0
        )
        for gx in range(8):
            row = h % GROUP * 64 + 8 * gx
            t1[h // GROUP, row : row + 8] = jnp.where(
                code1[8 * gx : 8 * gx + 8] == 1, pltpu.roll(two, 4 * gx, 1, stride=1, stride_axis=0), NEG
            )


def near_kernel(
    pos, own_hbm, wconv_hbm, wqkv_hbm, wout_hbm, send_hbm, up, down, left, right, pick, bconv, gain0,
    shift0, gains, shifts, bqkv, table, krow, kcol, qsel, bout, out, cat, x0s, ys, ks, vs, yq, xq, qs,
    att, own, wconv, wqkv, wout, send, extra, sems,
):
    copies = [
        pltpu.make_async_copy(src, dst, sems.at[i])
        for i, (src, dst) in enumerate(
            (
                (own_hbm, own), (wconv_hbm, wconv), (wqkv_hbm.at[0], wqkv), (wout_hbm.at[0], wout),
                (send_hbm, send),
            )
        )
    ]
    for copy in copies:
        copy.start()
    yi, xi, ysize, xsize = pos[0], pos[1], pos[3], pos[4]
    top = jnp.where(yi == 0, 0.0, 1.0).astype(BF16)
    side = jnp.where(xi == 0, 0.0, 1.0).astype(BF16)
    rows, cols = krow[...] + yi * TR, kcol[...] + xi * TC
    inside = (rows >= 0) & (rows < ysize * TR) & (cols >= 0) & (cols < xsize * TC)
    extra[...] = jnp.where(inside, 0.0, NEG)
    copies[0].wait()

    def main_row(e):
        if e < 7:
            row = up[e]
            return row * top if e == 6 else row
        return own[e - 7] if e < 39 else down[e - 39]

    def left_row(e):
        row = left[e] * side
        return row * top if e == 6 else row

    def right_row(e):
        return right[e] * top if e == 6 else right[e]

    for p in range(PAIRS):
        for a in range(3):
            e0, e1 = 4 * p + a, 4 * p + a + 2
            rows = jnp.concatenate(
                [main_row(e0), main_row(e1), left_row(e0), left_row(e1), right_row(e0), right_row(e1)],
                axis=0,
            )
            got = jnp.dot(pick[...], rows, preferred_element_type=F32).astype(BF16)
            for b in range(3):
                cat[PT * p : PT * p + PT, 256 * (3 * a + b) : 256 * (3 * a + b) + 256] = got[
                    PT * b : PT * b + PT
                ]
    copies[1].wait()
    conv = jnp.dot(cat[...], wconv[...], preferred_element_type=F32) + bconv[...]
    x0 = norm(conv, gain0[...], shift0[...]).astype(BF16)
    y = norm(x0.astype(F32), gains[0:1], shifts[0:1]).astype(BF16)
    x0s[...] = x0.reshape(PAIRS, PT, C3)
    ys[...] = y.reshape(PAIRS, PT, C3)
    copies[2].wait()
    kv = jnp.dot(y, wqkv[:, C3:], preferred_element_type=F32) + bqkv[0:1, C3:]
    ks[...] = kv[:, :C3].astype(BF16).reshape(PAIRS, PT, C3)
    vs[...] = kv[:, C3:].astype(BF16).reshape(PAIRS, PT, C3)

    def window(ref, m, h):
        part = ref[pl.ds(2 * m, 5), 32 * h : 32 * h + 48, :].reshape(240, C3)
        return jnp.concatenate([part, part[:16]], axis=0)

    for m in range(4):
        for h in range(2):
            at = slice((2 * m + h) * 64, (2 * m + h) * 64 + 64)
            sel = qsel[h]
            yq[at] = jnp.dot(sel, window(ys, m, h), preferred_element_type=F32).astype(BF16)
            xq[at] = jnp.dot(sel, window(x0s, m, h), preferred_element_type=F32)
    qs[...] = (
        jnp.dot(yq[...], wqkv[:, :C3], preferred_element_type=F32) + bqkv[0:1, :C3]
    ).astype(BF16)

    def block(m, _):
        for h in range(2):
            at = pl.ds(pl.multiple_of((2 * m + h) * 64, 64), 64)
            o = attend_block(
                qs[at], window(ks, m, h), window(vs, m, h), lambda g: table[h, g],
                extra[pl.ds(2 * m + h, 1), :],
            )
            att[at] = o.astype(BF16)
        return 0

    lax.fori_loop(0, 4, block, 0)
    copies[3].wait()
    copies[4].wait()
    x1 = jnp.dot(att[...], wout[...], preferred_element_type=F32) + bout[0:1] + xq[...]
    out[...] = jnp.dot(send[...], x1.astype(BF16), preferred_element_type=F32).astype(BF16)


def far_kernel(
    pos, wqkv_hbm, wout_hbm, above, own, below, gains, shifts, bqkv, ksel, table, bout, out, ys, yk, ks,
    vs, qs, att, wqkv, wout, sems,
):
    copies = [
        pltpu.make_async_copy(src, dst, sems.at[i])
        for i, (src, dst) in enumerate(((wqkv_hbm.at[1], wqkv), (wout_hbm.at[1], wout)))
    ]
    for copy in copies:
        copy.start()
    zi, zsize = pos[2], pos[5]
    for ref, at, n in ((above, 0, 128), (own, 128, 512), (below, 640, 128)):
        ys[at : at + n] = norm(ref[...].astype(F32), gains[1:2], shifts[1:2]).astype(BF16)
    for j in range(PAIRS):
        yk[64 * j : 64 * j + 64] = jnp.dot(
            ksel[...], ys[64 * j : 64 * j + 128], preferred_element_type=F32
        ).astype(BF16)
    copies[0].wait()
    kv = jnp.dot(yk[...], wqkv[:, C3:], preferred_element_type=F32) + bqkv[1:2, C3:]
    ks[...] = kv[:, :C3].astype(BF16)
    vs[...] = kv[:, C3:].astype(BF16)
    qs[...] = (
        jnp.dot(ys[128:640], wqkv[:, :C3], preferred_element_type=F32) + bqkv[1:2, :C3]
    ).astype(BF16)
    key_row = lax.broadcasted_iota(jnp.int32, (1, 256), 1) // 32 - 3

    def block(i, _):
        for u in range(2):
            m = 2 * i + u
            row = key_row + (16 * zi + 2 * m)
            extra = jnp.where((row >= 0) & (row < 16 * zsize), 0.0, NEG)
            at = pl.ds(pl.multiple_of(m * 64, 64), 64)
            keys = pl.ds(pl.multiple_of(m * 64, 64), 256)
            o = attend_block(qs[at], ks[keys], vs[keys], lambda g: table[g], extra)
            att[at] = o.astype(BF16)
        return 0

    lax.fori_loop(0, 4, block, 0)
    copies[1].wait()
    x2 = jnp.dot(att[...], wout[...], preferred_element_type=F32) + bout[1:2]
    out[...] = (x2 + own[...].astype(F32)).astype(BF16)


def back_kernel(got, sel, out):
    for i in range(8):
        rows = jnp.dot(sel[...], got[64 * i : 64 * i + 64], preferred_element_type=F32).astype(BF16)
        out[i] = rows[:32]
        out[8 + i] = rows[32:]


def call(kernel, out_shapes, scratch, args, smem=0, hbm=0, sems=0, flops=0):
    specs = [pl.BlockSpec(memory_space=pltpu.SMEM)] * smem
    specs += [pl.BlockSpec(memory_space=pltpu.HBM)] * hbm
    specs += [pl.BlockSpec(memory_space=pltpu.VMEM)] * (len(args) - smem - hbm)
    shapes = [pltpu.VMEM(s, t) for s, t in scratch]
    if sems:
        shapes.append(pltpu.SemaphoreType.DMA((sems,)))
    return pl.pallas_call(
        kernel,
        out_shape=[jax.ShapeDtypeStruct(s, t) for s, t in out_shapes],
        in_specs=specs,
        out_specs=[pl.BlockSpec(memory_space=pltpu.VMEM)] * len(out_shapes),
        scratch_shapes=shapes,
        compiler_params=pltpu.CompilerParams(vmem_limit_bytes=VMEM_LIMIT),
        cost_estimate=pl.CostEstimate(flops=flops, bytes_accessed=4 * 2**20, transcendentals=0),
    )(*args)


def build_tables(rel):
    hot0, code0 = near_patterns()
    hot1, code1 = far_patterns()
    return call(
        table_kernel,
        [((2, 2, GROUP * 64, 256), F32), ((2, GROUP * 64, 256), F32)],
        [],
        [rel, bf(hot0), jnp.asarray(code0), bf(hot1), jnp.asarray(code1)],
        flops=3 * 10**9,
    )


def near_call(pos, fmap, wconv, wqkv, wout, up, down, left, right, bconv, gain0, shift0, gains, shifts, bqkv, table, bout):
    krow, kcol = near_keys()
    rows = np.repeat(np.arange(4) * 4, 2)[:, None] + np.tile(krow, (4, 1)) - 3
    cols = np.tile(np.arange(2) * 16, 4)[:, None] + np.tile(kcol, (4, 1)) - 3
    tok = ((PAIRS, PT, C3), BF16)
    (x1,) = call(
        near_kernel,
        [((512, C3), BF16)],
        [
            ((NTOK, 9 * C2), BF16), tok, tok, tok, tok, ((512, C3), BF16), ((512, C3), F32),
            ((512, C3), BF16), ((512, C3), BF16), ((32, 64, C2), BF16), ((9 * C2, C3), BF16),
            ((C3, 3 * C3), BF16), ((C3, C3), BF16), ((512, 512), BF16), ((8, 256), F32),
        ],
        [
            pos, fmap, wconv.reshape(9 * C2, C3), wqkv, wout, bf(send_matrix()), up, down, left, right,
            bf(pick_matrix()), bconv.reshape(1, C3), gain0.reshape(1, C3), shift0.reshape(1, C3), gains,
            shifts, bqkv, table, jnp.asarray(rows), jnp.asarray(cols), bf(query_matrix()), bout,
        ],
        smem=1, hbm=5, sems=5, flops=10**10,
    )
    return x1


def far_call(pos, wqkv, wout, above, got, below, gains, shifts, bqkv, table, bout):
    (x2,) = call(
        far_kernel,
        [((512, C3), BF16)],
        [
            ((768, C3), BF16), ((704, C3), BF16), ((704, C3), BF16), ((704, C3), BF16),
            ((512, C3), BF16), ((512, C3), BF16), ((C3, 3 * C3), BF16), ((C3, C3), BF16),
        ],
        [pos, wqkv, wout, above, got, below, gains, shifts, bqkv, bf(far_key_matrix()), table, bout],
        smem=1, hbm=2, sems=2, flops=8 * 10**9,
    )
    return x2


def per_device(
    zsize, isize, xsize,
    fmap, wconv, bconv, gain0, shift0, gains, shifts, wqkv, bqkv, rel, wout, bout,
):
    zi, ii, xi = lax.axis_index("gz"), lax.axis_index("gi"), lax.axis_index("gx")
    ysize = zsize * isize
    yi = zi * isize + ii
    pos = jnp.stack([yi, xi, zi, ysize, xsize, zsize]).astype(jnp.int32)

    def shifted(x, dy, dx):
        pairs = [
            (y * xsize + c, ((y + dy) % ysize) * xsize + (c + dx) % xsize)
            for y in range(ysize)
            for c in range(xsize)
        ]
        return lax.ppermute(x, ("gz", "gi", "gx"), pairs)

    up = shifted(fmap[25:], 1, 0)
    down = shifted(fmap[:6], -1, 0)
    table0, table1 = build_tables(rel)

    def strip(at):
        return jnp.concatenate([up[:, at], fmap[:, at], down[:, at]], axis=0)

    left = shifted(strip(slice(56, 64)), 0, 1)
    right = shifted(strip(slice(0, 8)), 0, -1)
    x1 = near_call(
        pos, fmap, wconv, wqkv, wout, up, down, left, right, bconv, gain0, shift0, gains, shifts, bqkv,
        table0, bout,
    )
    got = lax.all_to_all(x1.reshape(64, 8, C3), ("gi", "gx"), 0, 0).reshape(512, C3)
    above = shifted(got[384:], isize, 0)
    below = shifted(got[:128], -isize, 0)
    x2 = far_call(pos, wqkv, wout, above, got, below, gains, shifts, bqkv, table1, bout)
    back = lax.all_to_all(x2.reshape(64, 8, C3), ("gi", "gx"), 0, 0).reshape(512, C3)
    (out,) = call(back_kernel, [((TR, TC, C3), BF16)], [], [back, bf(back_matrix())], flops=10**8)
    return out


def solution(mesh):
    gy, gx = mesh.shape["gy"], mesh.shape["gx"]
    inner = Mesh(mesh.devices.reshape(gy // 8, 8, gx), ("gz", "gi", "gx"))
    tile = P(("gz", "gi"), "gx", None)
    placed = (tile,) + (P(),) * 11
    return jax.shard_map(
        functools.partial(per_device, gy // 8, 8, gx),
        mesh=inner,
        in_specs=placed,
        out_specs=tile,
        check_vma=False,
    )
```

time: 118 us -> 101 us (0.86)
  blocking collectives: 17.9 us -> 48.6 us
  starting transfers between devices: 23.6 us -> 9.56 us
  matrix products: 11.6 us -> 0 us
  local copies, waits for them, and re-layouts: 14.5 us -> 3.2 us
  Pallas kernels: 30.5 us -> 24 us
  waiting for transfers between devices: 17.4 us -> 15 us
  other arithmetic: 2.2 us -> 0.05 us
    all_to_all x0 -> x1, blocking collectives: none -> 30.8 us  [per_device(): lax.all_to_all(x1.reshape(64, 8, C3), ('gi', 'gx'), 0, 0).reshape(512, C3)]
    all_to_all x1 -> x0, starting transfers between devices: 12.6 us -> none  [per_device(): lax.all_to_all(x1.reshape(64, 8, C3), ('gi', 'gx'), 0, 0).reshape(512, C3)]
    dot_general x2 -> x0, matrix products: 11.6 us -> none  [tables(): jnp.einsum('ho,o...->h...', rel[layer], jnp.asarray(hot), precision=lax.P...]
    pallas_call x3 -> x4, Pallas kernels: 30.5 us -> 24 us  [call(): pl.pallas_call(kernel, out_shape=[jax.ShapeDtypeStruct(s, t) for s, t in...]
    all_to_all x1 -> x0, waiting for transfers between devices: 6.24 us -> none  [per_device(): lax.all_to_all(x1.reshape(64, 8, C3), ('gi', 'gx'), 0, 0).reshape(512, C3)]
    squeeze x2 -> x0, local copies, waits for them, and re-layouts: 4.92 us -> none  [the longest x1 3.88 us: per_device(): wqkv[1]]
    select_n x2 -> x0, local copies, waits for them, and re-layouts: 4.15 us -> none  [tables(): return jnp.where(jnp.asarray(near)[None], t * LOG2E, NEG)]
    ppermute x6, waiting for transfers between devices: 11.2 us -> 15 us  [shifted(): return lax.ppermute(x, ('gz', 'gi', 'gx'), pairs)]
  transfers between devices with their start and end apart: 7 -> 6, of which waited for: 4 -> 6; matrix products, arithmetic and copies ran while one was open for 22% -> 2% of each run, Pallas kernels for 0% -> 2%
where the time goes in v1:
time: 101 us
  blocking collectives  48.6 us (48%)
  Pallas kernels  24 us (24%)
  waiting for transfers between devices  15 us (15%)
  starting transfers between devices  9.56 us (9%)
  local copies, waits for them, and re-layouts  3.2 us (3%)
    all_to_all x1, blocking collectives, per_device(): lax.all_to_all(x1.reshape(64, 8, C3), ('gi', 'gx'), 0, 0).reshape(512, C3)  30.8 us
    pallas_call x4, Pallas kernels, call(): pl.pallas_call(kernel, out_shape=[jax.ShapeDtypeStruct(s, t) for s, t in...  24 us
    all_to_all x1, blocking collectives, per_device(): lax.all_to_all(x2.reshape(64, 8, C3), ('gi', 'gx'), 0, 0).reshape(512, C3)  17.9 us
    ppermute x6, waiting for transfers between devices, shifted(): return lax.ppermute(x, ('gz', 'gi', 'gx'), pairs)  15 us
    ppermute x6, starting transfers between devices, shifted(): return lax.ppermute(x, ('gz', 'gi', 'gx'), pairs)  9.56 us
  transfers between devices with their start and end apart: 6, of which 6 were waited for; matrix products, arithmetic and copies ran while one was open for 2% of the time, Pallas kernels for 2%

profile of v1, /device:TPU:1, one launch (start us, length us, event | category | flops | bytes accessed | tf_op | source)
XLA Modules:
  0.0 100.8 jit_solution(5244198442356181356)
XLA Ops:
  0.0 0.0 copy-start.14
  0.0 1.0 slice.37
  1.0 3.3 %collective-permute-start.1 = (bf16[6,64,256]{2,1,0:T(8,128)(2,1)S(1)}, bf16[6,64,256]{2,1,0:T(8,128)(2,1)S(1)}, u32[]{:S(2)}, u32[]{:S(2)}) collective-permute-start(bf16[6,64,256]{2,1,0:T(8,128)(2,1)S(1)} %slice.37), channel_id=1, source_target_pairs={{0,248},{1,249},{2,250},{3,251},{4,252},{5,253},{6,254},{7,255},{8... | collective-permute-start | bytes 589832 | tf_op jit(solution)/shard_map/ppermute | solution.py:434
  4.3 1.0 slice.36
  5.3 0.1 collective-permute-start
  5.4 1.0 fusion
  6.4 0.1 stack.15.pos
  6.5 0.7 collective-permute-done.1.down
  7.2 5.7 %collective-permute-done.up = bf16[7,64,256]{2,1,0:T(8,128)(2,1)S(1)} collective-permute-done((bf16[7,64,256]{2,1,0:T(8,128)(2,1)S(1)}, bf16[7,64,256]{2,1,0:T(8,128)(2,1)S(1)}, u32[]{:S(2)}, u32[]{:S(2)}) %collective-permute-start) | collective-permute-done | bytes 229408 | tf_op jit(solution)/shard_map/ppermute | solution.py:434
  12.9 0.8 collective-permute-start.2
  13.7 0.0 copy-start
  13.7 0.0 copy-start.4
  13.8 0.0 copy-start.6
  13.8 0.0 copy-start.13
  13.9 0.0 copy-start.16
  13.9 0.0 copy-start.17
  13.9 0.0 copy-start.21
  13.9 0.0 copy-start.22
  13.9 2.9 %collective-permute-start.3 = (bf16[45,8,256]{2,1,0:T(8,128)(2,1)S(1)}, bf16[45,8,256]{2,1,0:T(8,128)(2,1)S(1)}, u32[]{:S(2)}, u32[]{:S(2)}) collective-permute-start(bf16[45,8,256]{2,1,0:T(8,128)(2,1)S(1)} %pad_maximum_fusion.1), channel_id=1, source_target_pairs={{0,7},{1,0},{2,1},{3,2},{4,3},{5,4},{6,5},{7,6},{8,15},{9,8},{10,9... | collective-permute-start | bytes 552968 | tf_op jit(solution)/shard_map/ppermute | solution.py:434
  16.8 1.7 %shard_map.217 = (f32[2,2,512,256]{3,2,1,0:T(8,128)S(1)}, f32[2,512,256]{2,1,0:T(8,128)S(1)}) custom-call(f32[2,16,49]{2,1,0:T(8,128)S(1)} %copy-done.5, bf16[49,4096]{1,0:T(8,128)(2,1)S(1)} %copy-done.14, s32[2,64,256]{2,1,0:T(8,128)S(1)} %copy-done.15, bf16[49,512]{1,0:T(8,128)(2,1)S(1)} %copy-done.19, s32[64,256]{1,0:T(8,128)S(1)} %copy-done.18), custom_call_target="tpu_custom_call" | custom-call | flops 3000000000 | bytes 4194304 | tf_op jit(solution)/shard_map/pallas_call | solution.py:359
  18.5 1.2 %collective-permute-done.2.left = bf16[45,8,256]{2,1,0:T(8,128)(2,1)S(1)} collective-permute-done((bf16[45,8,256]{2,1,0:T(8,128)(2,1)S(1)}, bf16[45,8,256]{2,1,0:T(8,128)(2,1)S(1)}, u32[]{:S(2)}, u32[]{:S(2)}) %collective-permute-start.2) | collective-permute-done | bytes 184352 | tf_op jit(solution)/shard_map/ppermute | solution.py:434
  19.7 0.8 collective-permute-done.3.right
  20.7 0.0 copy-start.20
  20.7 13.2 %shard_map.218 = bf16[512,512]{1,0:T(8,128)(2,1)S(1)} custom-call(s32[6]{0:T(128)S(1)} %stack.15.pos, bf16[32,64,256]{2,1,0:T(8,128)(2,1)S(1)} %copy-done, bf16[2304,512]{1,0:T(8,128)(2,1)S(1)} %bitcast.19, bf16[2,512,1536]{2,1,0:T(8,128)(2,1)S(1)} %copy-done.2, bf16[2,512,512]{2,1,0:T(8,128)(2,1)S(1)} %copy-done.4, bf16[512,512]{1,0:T(8,128)(2,1)S(1)} %copy-done.13, ...), custom_call_target="tpu_custom_call" | custom-call | flops 10000000000 | bytes 4194304 | tf_op jit(solution)/shard_map/pallas_call | solution.py:359
  33.9 30.8 %all_to_all.10 = bf16[64,8,512]{2,1,0:T(8,128)(2,1)S(1)} all-to-all(bf16[64,8,512]{2,1,0:T(8,128)(2,1)S(1)} %bitcast.17), channel_id=1, replica_groups=mesh['gz'=4,'gi'=8,'gx'=8] {'gi','gx'}, dimensions={0} | all-to-all | bytes 1048576 | tf_op jit(solution)/shard_map/all_to_all | solution.py:449
  64.7 0.5 collective-permute-start.5
  65.2 2.0 %collective-permute-start.4 = (bf16[128,512]{1,0:T(8,128)(2,1)S(1)}, bf16[128,512]{1,0:T(8,128)(2,1)S(1)}, u32[]{:S(2)}, u32[]{:S(2)}) collective-permute-start(bf16[128,512]{1,0:T(8,128)(2,1)S(1)} %get-tuple-element.12), channel_id=1, source_target_pairs={{0,64},{1,65},{2,66},{3,67},{4,68},{5,69},{6,70},{7,71},{8,72},{9,... | collective-permute-start | bytes 393224 | tf_op jit(solution)/shard_map/ppermute | solution.py:434
  67.2 5.4 %collective-permute-done.5.below = bf16[128,512]{1,0:T(8,128)(2,1)S(1)} collective-permute-done((bf16[128,512]{1,0:T(8,128)(2,1)S(1)}, bf16[128,512]{1,0:T(8,128)(2,1)S(1)}, u32[]{:S(2)}, u32[]{:S(2)}) %collective-permute-start.5) | collective-permute-done | bytes 131104 | tf_op jit(solution)/shard_map/ppermute | solution.py:434
  72.6 1.2 %collective-permute-done.4.above = bf16[128,512]{1,0:T(8,128)(2,1)S(1)} collective-permute-done((bf16[128,512]{1,0:T(8,128)(2,1)S(1)}, bf16[128,512]{1,0:T(8,128)(2,1)S(1)}, u32[]{:S(2)}, u32[]{:S(2)}) %collective-permute-start.4) | collective-permute-done | bytes 131104 | tf_op jit(solution)/shard_map/ppermute | solution.py:434
  73.8 8.0 %shard_map.219 = bf16[512,512]{1,0:T(8,128)(2,1)S(1)} custom-call(s32[6]{0:T(128)S(1)} %stack.15.pos, bf16[2,512,1536]{2,1,0:T(8,128)(2,1)S(1)} %copy-done.2, bf16[2,512,512]{2,1,0:T(8,128)(2,1)S(1)} %copy-done.4, bf16[128,512]{1,0:T(8,128)(2,1)S(1)} %collective-permute-done.4.above, bf16[512,512]{1,0:T(8,128)(2,1)S(1)} %bitcast.16, ...), custom_call_target="tpu_custom_call" | custom-call | flops 8000000000 | bytes 4194304 | tf_op jit(solution)/shard_map/pallas_call | solution.py:359
  81.8 17.9 %all_to_all.11 = bf16[64,8,512]{2,1,0:T(8,128)(2,1)S(1)} all-to-all(bf16[64,8,512]{2,1,0:T(8,128)(2,1)S(1)} %bitcast.18), channel_id=1, replica_groups=mesh['gz'=4,'gi'=8,'gx'=8] {'gi','gx'}, dimensions={0} | all-to-all | bytes 1048576 | tf_op jit(solution)/shard_map/all_to_all | solution.py:453
  99.7 1.1 %shard_map.220 = bf16[16,32,512]{2,1,0:T(8,128)(2,1)} custom-call(bf16[512,512]{1,0:T(8,128)(2,1)S(1)} %bitcast.15, bf16[64,64]{1,0:T(8,128)(2,1)S(1)} %copy-done.1), custom_call_target="tpu_custom_call" | custom-call | flops 100000000 | bytes 4194304 | tf_op jit(solution)/shard_map/pallas_call | solution.py:359
  (41 shorter events, 0.2 us)
Async XLA Ops:
  0.0 16.8 %copy-start.18 = (s32[64,256]{1,0:T(8,128)S(1)}, s32[64,256]{1,0:T(8,128)}, u32[]{:S(2)}) copy-start(s32[64,256]{1,0:T(8,128)} %constant.45.clone.code1) | copy-start | bytes 196612
  0.0 16.8 %copy-start.19 = (bf16[49,512]{1,0:T(8,128)(2,1)S(1)}, bf16[49,512]{1,0:T(8,128)(2,1)}, u32[]{:S(2)}) copy-start(bf16[49,512]{1,0:T(8,128)(2,1)} %constant.44.clone.hot1) | copy-start | bytes 150532
  0.0 16.8 %copy-start.15 = (s32[2,64,256]{2,1,0:T(8,128)S(1)}, s32[2,64,256]{2,1,0:T(8,128)}, u32[]{:S(2)}) copy-start(s32[2,64,256]{2,1,0:T(8,128)} %constant.43.clone.code0) | copy-start | bytes 393220
  0.0 16.8 %copy-start.14 = (bf16[49,4096]{1,0:T(8,128)(2,1)S(1)}, bf16[49,4096]{1,0:T(8,128)(2,1)}, u32[]{:S(2)}) copy-start(bf16[49,4096]{1,0:T(8,128)(2,1)} %constant.42.clone.hot0) | copy-start | bytes 1204228
  0.0 16.8 %copy-start.5 = (f32[2,16,49]{2,1,0:T(8,128)S(1)}, f32[2,16,49]{2,1,0:T(8,128)}, u32[]{:S(2)}) copy-start(f32[2,16,49]{2,1,0:T(8,128)} %rel.1) | copy-start | bytes 18820
  1.0 6.1 %collective-permute-start.1 = (bf16[6,64,256]{2,1,0:T(8,128)(2,1)S(1)}, bf16[6,64,256]{2,1,0:T(8,128)(2,1)S(1)}, u32[]{:S(2)}, u32[]{:S(2)}) collective-permute-start(bf16[6,64,256]{2,1,0:T(8,128)(2,1)S(1)} %slice.37), channel_id=1, source_target_pairs={{0,248},{1,249},{2,250},{3,251},{4,252},{5,253},{6,254},{7,255},{8... | collective-permute-start | bytes 589832 | tf_op jit(solution)/shard_map/ppermute | solution.py:434
  5.3 7.5 %collective-permute-start = (bf16[7,64,256]{2,1,0:T(8,128)(2,1)S(1)}, bf16[7,64,256]{2,1,0:T(8,128)(2,1)S(1)}, u32[]{:S(2)}, u32[]{:S(2)}) collective-permute-start(bf16[7,64,256]{2,1,0:T(8,128)(2,1)S(1)} %slice.36), channel_id=1, source_target_pairs={{0,8},{1,9},{2,10},{3,11},{4,12},{5,13},{6,14},{7,15},{8,16},{9,17... | collective-permute-start | bytes 688136 | tf_op jit(solution)/shard_map/ppermute | solution.py:434
  12.9 6.9 %collective-permute-start.2 = (bf16[45,8,256]{2,1,0:T(8,128)(2,1)S(1)}, bf16[45,8,256]{2,1,0:T(8,128)(2,1)S(1)}, u32[]{:S(2)}, u32[]{:S(2)}) collective-permute-start(bf16[45,8,256]{2,1,0:T(8,128)(2,1)S(1)} %pad_maximum_fusion), channel_id=1, source_target_pairs={{0,1},{1,2},{2,3},{3,4},{4,5},{5,6},{6,7},{7,0},{8,9},{9,10},{10,1... | collective-permute-start | bytes 552968 | tf_op jit(solution)/shard_map/ppermute | solution.py:434
  13.7 6.8 %copy-start = (bf16[32,64,256]{2,1,0:T(8,128)(2,1)S(1)}, bf16[32,64,256]{2,1,0:T(8,128)(2,1)}, u32[]{:S(2)}) copy-start(bf16[32,64,256]{2,1,0:T(8,128)(2,1)} %own_hbm.1) | copy-start | bytes 3145732
  13.7 6.8 %copy-start.2 = (bf16[2,512,1536]{2,1,0:T(8,128)(2,1)S(1)}, bf16[2,512,1536]{2,1,0:T(8,128)(2,1)}, u32[]{:S(2)}) copy-start(bf16[2,512,1536]{2,1,0:T(8,128)(2,1)} %wqkv_hbm.3) | copy-start | bytes 9437188
  13.7 6.8 %copy-start.3 = (bf16[3,3,256,512]{3,2,1,0:T(8,128)(2,1)S(1)}, bf16[3,3,256,512]{3,2,1,0:T(8,128)(2,1)}, u32[]{:S(2)}) copy-start(bf16[3,3,256,512]{3,2,1,0:T(8,128)(2,1)} %param.24) | copy-start | bytes 7077892
  13.7 6.8 %copy-start.4 = (bf16[2,512,512]{2,1,0:T(8,128)(2,1)S(1)}, bf16[2,512,512]{2,1,0:T(8,128)(2,1)}, u32[]{:S(2)}) copy-start(bf16[2,512,512]{2,1,0:T(8,128)(2,1)} %wout_hbm.3) | copy-start | bytes 3145732
  13.8 6.8 %copy-start.6 = (f32[2,1536]{1,0:T(2,128)S(1)}, f32[2,1536]{1,0:T(2,128)}, u32[]{:S(2)}) copy-start(f32[2,1536]{1,0:T(2,128)} %bqkv.3) | copy-start | bytes 36868
  13.8 6.8 %copy-start.7 = (f32[2,512]{1,0:T(2,128)S(1)}, f32[2,512]{1,0:T(2,128)}, u32[]{:S(2)}) copy-start(f32[2,512]{1,0:T(2,128)} %gains.3) | copy-start | bytes 12292
  13.8 6.8 %copy-start.8 = (f32[2,512]{1,0:T(2,128)S(1)}, f32[2,512]{1,0:T(2,128)}, u32[]{:S(2)}) copy-start(f32[2,512]{1,0:T(2,128)} %shifts.3) | copy-start | bytes 12292
  13.8 6.8 %copy-start.9 = (f32[2,512]{1,0:T(2,128)S(1)}, f32[2,512]{1,0:T(2,128)}, u32[]{:S(2)}) copy-start(f32[2,512]{1,0:T(2,128)} %bout.3) | copy-start | bytes 12292
  13.8 6.8 %copy-start.10 = (f32[512]{0:T(512)S(1)}, f32[512]{0:T(512)}, u32[]{:S(2)}) copy-start(f32[512]{0:T(512)} %param.25) | copy-start | bytes 6148
  13.8 6.8 %copy-start.11 = (f32[512]{0:T(512)S(1)}, f32[512]{0:T(512)}, u32[]{:S(2)}) copy-start(f32[512]{0:T(512)} %param.26) | copy-start | bytes 6148
  13.8 6.8 %copy-start.12 = (f32[512]{0:T(512)S(1)}, f32[512]{0:T(512)}, u32[]{:S(2)}) copy-start(f32[512]{0:T(512)} %param.27) | copy-start | bytes 6148
  13.8 6.8 %copy-start.13 = (bf16[512,512]{1,0:T(8,128)(2,1)S(1)}, bf16[512,512]{1,0:T(8,128)(2,1)}, u32[]{:S(2)}) copy-start(bf16[512,512]{1,0:T(8,128)(2,1)} %constant.46.clone.send_hbm) | copy-start | bytes 1572868
  13.9 6.8 %copy-start.16 = (bf16[240,160]{1,0:T(8,128)(2,1)S(1)}, bf16[240,160]{1,0:T(8,128)(2,1)}, u32[]{:S(2)}) copy-start(bf16[240,160]{1,0:T(8,128)(2,1)} %constant.47.clone.pick) | copy-start | bytes 230404
  13.9 6.8 %copy-start.17 = (bf16[2,64,256]{2,1,0:T(8,128)(2,1)S(1)}, bf16[2,64,256]{2,1,0:T(8,128)(2,1)}, u32[]{:S(2)}) copy-start(bf16[2,64,256]{2,1,0:T(8,128)(2,1)} %constant.50.clone.qsel) | copy-start | bytes 196612
  13.9 6.8 %copy-start.21 = (s32[8,256]{1,0:T(8,128)S(1)}, s32[8,256]{1,0:T(8,128)}, u32[]{:S(2)}) copy-start(s32[8,256]{1,0:T(8,128)} %constant.49.clone.kcol) | copy-start | bytes 24580
  13.9 6.8 %copy-start.22 = (s32[8,256]{1,0:T(8,128)S(1)}, s32[8,256]{1,0:T(8,128)}, u32[]{:S(2)}) copy-start(s32[8,256]{1,0:T(8,128)} %constant.48.clone.krow) | copy-start | bytes 24580
  13.9 6.6 %collective-permute-start.3 = (bf16[45,8,256]{2,1,0:T(8,128)(2,1)S(1)}, bf16[45,8,256]{2,1,0:T(8,128)(2,1)S(1)}, u32[]{:S(2)}, u32[]{:S(2)}) collective-permute-start(bf16[45,8,256]{2,1,0:T(8,128)(2,1)S(1)} %pad_maximum_fusion.1), channel_id=1, source_target_pairs={{0,7},{1,0},{2,1},{3,2},{4,3},{5,4},{6,5},{7,6},{8,15},{9,8},{10,9... | collective-permute-start | bytes 552968 | tf_op jit(solution)/shard_map/ppermute | solution.py:434
  20.7 53.2 %copy-start.20 = (bf16[64,128]{1,0:T(8,128)(2,1)S(1)}, bf16[64,128]{1,0:T(8,128)(2,1)}, u32[]{:S(2)}) copy-start(bf16[64,128]{1,0:T(8,128)(2,1)} %constant.51.clone.ksel) | copy-start | bytes 49156
  64.7 7.9 %collective-permute-start.5 = (bf16[128,512]{1,0:T(8,128)(2,1)S(1)}, bf16[128,512]{1,0:T(8,128)(2,1)S(1)}, u32[]{:S(2)}, u32[]{:S(2)}) collective-permute-start(bf16[128,512]{1,0:T(8,128)(2,1)S(1)} %get-tuple-element.11), channel_id=1, source_target_pairs={{0,192},{1,193},{2,194},{3,195},{4,196},{5,197},{6,198},{7,199},{8... | collective-permute-start | bytes 393224 | tf_op jit(solution)/shard_map/ppermute | solution.py:434
  65.2 8.7 %collective-permute-start.4 = (bf16[128,512]{1,0:T(8,128)(2,1)S(1)}, bf16[128,512]{1,0:T(8,128)(2,1)S(1)}, u32[]{:S(2)}, u32[]{:S(2)}) collective-permute-start(bf16[128,512]{1,0:T(8,128)(2,1)S(1)} %get-tuple-element.12), channel_id=1, source_target_pairs={{0,64},{1,65},{2,66},{3,67},{4,68},{5,69},{6,70},{7,71},{8,72},{9,... | collective-permute-start | bytes 393224 | tf_op jit(solution)/shard_map/ppermute | solution.py:434
  73.8 25.8 %copy-start.1 = (bf16[64,64]{1,0:T(8,128)(2,1)S(1)}, bf16[64,64]{1,0:T(8,128)(2,1)}, u32[]{:S(2)}) copy-start(bf16[64,64]{1,0:T(8,128)(2,1)} %constant.52.clone.sel) | copy-start | bytes 24580

commit v2 on v1

v2 whole, which is shorter than its diff:
```python
import functools

import jax
import jax.numpy as jnp
import ml_dtypes
import numpy as np
from jax import lax
from jax.experimental import pallas as pl
from jax.experimental.pallas import tpu as pltpu
from jax.sharding import Mesh, PartitionSpec as P

F32 = jnp.float32
BF16 = jnp.bfloat16
KERNEL = 7
HALF = 3
NEG = -1e30
LOG2E = 1.4426950408889634
TR, TC = 16, 32
C2, C3 = 256, 512
HEADS, HD = 16, 32
GROUP = 8
DIL = 8
PAIRS = 11
PT = 80
NTOK = PAIRS * PT
EPS = 1e-5
VMEM_TABLE, VMEM_NEAR, VMEM_FAR, VMEM_BACK = 56, 48, 46, 46


def pair_slots():
    out = []
    for rp in range(2):
        for c in range(16):
            out.append((rp * 16 + c, rp, c))
        for c in range(16, 22):
            out.append((32 + rp * 8 + c - 16, rp, c))
        for c in range(22, 38):
            out.append((48 + rp * 16 + c - 22, rp, c))
    return out


def pick_matrix():
    pick = np.zeros((3 * PT, 160), np.float32)
    for b in range(3):
        for slot, rp, c in pair_slots():
            col = 2 * c + b - 7
            if col < 0:
                k = 128 + 16 * rp + col + 8
            elif col < 64:
                k = 64 * rp + col
            else:
                k = 136 + 16 * rp + col - 64
            pick[b * PT + slot, k] = 1
    return pick


def near_keys():
    rows = np.full((2, 256), -99, np.int32)
    cols = np.full((2, 256), -99, np.int32)
    for half in range(2):
        for j in range(5):
            for slot, rp, c in pair_slots():
                at = slot - 32 * half
                if 0 <= at < 48:
                    rows[half, 48 * j + at] = 2 * j + rp
                    cols[half, 48 * j + at] = c - 16 * half
    return rows, cols


def query_matrix():
    rows, cols = near_keys()
    sel = np.zeros((2, 64, 256), np.float32)
    for half in range(2):
        for k in range(256):
            r, c = rows[half, k] - 3, cols[half, k] - 3
            if 0 <= r < 4 and 0 <= c < 16:
                sel[half, r * 16 + c, k] = 1
    return sel


def near_patterns():
    rows, cols = near_keys()
    hot = np.zeros((49, 2, 2, 4, 256), np.float32)
    code = np.zeros((2, 64, 256), np.int32)
    for half in range(2):
        for k in range(256):
            if rows[half, k] < 0:
                continue
            wide = (cols[half, k] < 16) if half == 0 else (cols[half, k] >= 6)
            for q in range(64):
                dr, dc = rows[half, k] - q // 16, cols[half, k] - q % 16
                if 0 <= dr < 7 and 0 <= dc < 7:
                    part = 0 if wide else 1
                    code[half, q, k] = 1 + part
                    hot[dr * 7 + dc, half, part, q // 16, (k - q % 16) % 256] = 1
    return hot.reshape(49, 4096), code


def far_patterns():
    hot = np.zeros((49, 2, 256), np.float32)
    code = np.zeros((64, 256), np.int32)
    for q in range(64):
        gx, a, b = q // 8, q % 8 // 4, q % 4
        for k in range(256):
            dr, dc = k // 32 - a, k % 32 - (4 * gx + b) + 3
            if 0 <= dr < 7 and 0 <= dc < 7:
                code[q, k] = 1
                hot[dr * 7 + dc, a, (k - 4 * gx - 4 * a - b) % 256] = 1
    return hot.reshape(49, 512), code


def send_matrix():
    perm = np.zeros((2, 256, 256), np.float32)
    for m in range(4):
        for h in range(2):
            for qr in range(4):
                for qc in range(16):
                    row, col = 4 * m + qr, 16 * h + qc
                    dst = ((row % 8) * 8 + col % 8) * 8 + (row // 8) * 4 + col // 8
                    src = (m // 2 * 2 + h) * 64 + qr * 16 + qc
                    perm[m % 2, dst - 256 * (m % 2), src] = 1
    return perm


def far_key_matrix():
    sel = np.zeros((64, 128), np.float32)
    for src in range(2):
        for gx in range(8):
            for a in range(2):
                for b in range(4):
                    if (src == 0) == (a == 1):
                        rp = src
                        sel[rp * 32 + gx * 4 + b, src * 64 + gx * 8 + a * 4 + b] = 1
    return sel


def back_matrix():
    sel = np.zeros((64, 64), np.float32)
    for j in range(8):
        for a in range(2):
            for b in range(4):
                sel[a * 32 + b * 8 + j, j * 8 + a * 4 + b] = 1
    return sel


def bf(x):
    return jnp.asarray(x.astype(ml_dtypes.bfloat16))


def norm(v, gain, shift):
    mean = jnp.mean(v, axis=-1, keepdims=True)
    d = v - mean
    var = jnp.mean(d * d, axis=-1, keepdims=True)
    return d * lax.rsqrt(var + EPS) * gain + shift


def attend_block(q, k, v, table, extra):
    lane = lax.broadcasted_iota(jnp.int32, (1, 256), 1) // HD
    outs = []
    for g in range(HEADS // GROUP):
        at = slice(256 * g, 256 * g + 256)
        qg, kg, vg = q[:, at], k[:, at], v[:, at]
        stacked = jnp.concatenate(
            [qg * (lane == h).astype(BF16) for h in range(GROUP)], axis=0
        )
        s = lax.dot_general(stacked, kg, (((1,), (1,)), ((), ())), preferred_element_type=F32)
        s = s + (table(g) if extra is None else table(g) + extra)
        peak = jnp.max(s, axis=-1, keepdims=True)
        p = jnp.exp2(s - peak)
        total = jnp.sum(p, axis=-1, keepdims=True)
        o = jnp.dot(p.astype(BF16), vg, preferred_element_type=F32) * (1.0 / total)
        for w in range(2):
            side = slice(128 * w, 128 * w + 128)
            acc = o[256 * w : 256 * w + 64, side]
            for h in range(1, 4):
                row = 64 * (4 * w + h)
                acc = jnp.where(lane[:, :128] == h, o[row : row + 64, side], acc)
            outs.append(acc)
    return jnp.concatenate(outs, axis=1).astype(BF16)


def project(x, w, bias):
    return jnp.dot(x, w, preferred_element_type=F32) + bias


def scaled(q):
    return (q * (HD**-0.5 * LOG2E)).astype(BF16)


def table_kernel(rel, hot0, code0, hot1, code1, t0, t1):
    def spread(r, hot):
        hi = r.astype(BF16)
        mid = (r - hi.astype(F32)).astype(BF16)
        lo = (r - hi.astype(F32) - mid.astype(F32)).astype(BF16)
        dot = functools.partial(jnp.dot, preferred_element_type=F32)
        return (dot(hi, hot[...]) + dot(mid, hot[...]) + dot(lo, hot[...])) * LOG2E

    e0 = spread(rel[0], hot0)
    e1 = spread(rel[1], hot1)
    for h in range(HEADS):
        for half in range(2):
            for qr in range(4):
                part = []
                for i in range(2):
                    at = ((half * 2 + i) * 4 + qr) * 256
                    one = jnp.broadcast_to(e0[h : h + 1, at : at + 256], (16, 256))
                    part.append(pltpu.roll(one, 0, 1, stride=1, stride_axis=0))
                code = code0[half, 16 * qr : 16 * qr + 16]
                row = h % GROUP * 64 + 16 * qr
                t0[half, h // GROUP, row : row + 16] = jnp.where(
                    code == 1, part[0], jnp.where(code == 2, part[1], NEG)
                )
        two = jnp.concatenate(
            [jnp.broadcast_to(e1[h : h + 1, 256 * a : 256 * a + 256], (4, 256)) for a in range(2)], axis=0
        )
        for gx in range(8):
            row = h % GROUP * 64 + 8 * gx
            t1[h // GROUP, row : row + 8] = jnp.where(
                code1[8 * gx : 8 * gx + 8] == 1, pltpu.roll(two, 4 * gx, 1, stride=1, stride_axis=0), NEG
            )


def start_copies(pairs, sems):
    copies = [pltpu.make_async_copy(src, dst, sems.at[i]) for i, (src, dst) in enumerate(pairs)]
    for copy in copies:
        copy.start()
    return copies


def conv_taps(cat, pick, pairs, main, rim):
    for i, p in enumerate(pairs):
        for a in range(3):
            e0, e1 = 4 * p + a, 4 * p + a + 2
            rows = jnp.concatenate([main(e0), main(e1), rim(e0), rim(e1)], axis=0)
            got = jnp.dot(pick[...], rows, preferred_element_type=F32).astype(BF16)
            for b in range(3):
                at = 256 * (3 * a + b)
                cat[PT * i : PT * i + PT, at : at + 256] = got[PT * b : PT * b + PT]


def rim_mask(pos):
    edge = jnp.where(pos[1] == 0, 0.0, 1.0)
    return jnp.where(lax.broadcasted_iota(jnp.int32, (16, C2), 0) < 8, edge, 1.0).astype(BF16)


def near_inside(pos, krow, kcol):
    rows, cols = krow[...] + pos[0] * TR, kcol[...] + pos[1] * TC
    inside = (rows >= 0) & (rows < pos[3] * TR) & (cols >= 0) & (cols < pos[4] * TC)
    return jnp.where(inside, 0.0, NEG)


def window(ref, first, h):
    part = ref[first : first + 5, 32 * h : 32 * h + 48, :].reshape(240, C3)
    return jnp.concatenate([part, part[:16]], axis=0)


def tokens_of(cat, wconv, wqkv, bconv, gain0, shift0, gains, shifts, bqkv):
    x0 = norm(project(cat, wconv[...], bconv[...]), gain0[...], shift0[...]).astype(BF16)
    y = norm(x0.astype(F32), gains[0:1], shifts[0:1]).astype(BF16)
    kv = project(y, wqkv[:, C3:], bqkv[0:1, C3:]).astype(BF16)
    return [t.reshape(-1, PT, C3) for t in (x0, y, kv[:, :C3], kv[:, C3:])]


def near_rows(firsts, blocks, x0, y, k, v, qsel, table, extra, wqkv, wout, bqkv, bout):
    yq, xq = [], []
    for first in firsts:
        for h in range(2):
            yq.append(jnp.dot(qsel[h], window(y, first, h), preferred_element_type=F32).astype(BF16))
            xq.append(jnp.dot(qsel[h], window(x0, first, h), preferred_element_type=F32))
    q = scaled(project(jnp.concatenate(yq, axis=0), wqkv[:, :C3], bqkv[0:1, :C3]))
    att = []
    for i, block in enumerate(blocks):
        first, h = firsts[i // 2], i % 2
        att.append(
            attend_block(
                q[64 * i : 64 * i + 64], window(k, first, h), window(v, first, h), lambda g: table[h, g],
                extra[block : block + 1],
            )
        )
    out = project(jnp.concatenate(att, axis=0), wout[...], bout[0:1]) + jnp.concatenate(xq, axis=0)
    return out.astype(BF16)


def near_first(
    pos, own_hbm, wconv_hbm, wqkv_hbm, wout_hbm, table_hbm, left, right, pick, bconv, gain0, shift0, gains,
    shifts, bqkv, bout, krow, kcol, qsel, x0s, ys, ks, vs, x1, cat, own, wconv, wqkv, wout, table, sems,
):
    copies = start_copies(
        (
            (own_hbm, own), (wconv_hbm, wconv), (wqkv_hbm.at[0], wqkv), (table_hbm, table),
            (wout_hbm.at[0], wout),
        ),
        sems,
    )
    mask = rim_mask(pos)
    extra = near_inside(pos, krow, kcol)
    copies[0].wait()

    def rim(e):
        return jnp.concatenate([left[e - 7], right[e - 7]], axis=0) * mask

    conv_taps(cat, pick, range(2, 9), lambda e: own[e - 7], rim)
    copies[1].wait()
    copies[2].wait()
    made = tokens_of(cat[...], wconv, wqkv, bconv, gain0, shift0, gains, shifts, bqkv)
    for ref, t in zip((x0s, ys, ks, vs), made):
        ref[...] = t
    copies[3].wait()
    copies[4].wait()
    x1[...] = near_rows(
        (0, 2), (2, 3, 4, 5), x0s, ys, ks, vs, qsel, table, extra, wqkv, wout, bqkv, bout
    )


def near_second(
    pos, own_hbm, wconv_hbm, wqkv_hbm, wout_hbm, table_hbm, up, down, left, right, x0s, ys, ks, vs, x1mid,
    pick, bconv, gain0, shift0, gains, shifts, bqkv, bout, krow, kcol, qsel, send, out, cat, x0b, yb, kb, vb,
    own, wconv, wqkv, wout, table, sems,
):
    held = [
        (src.at[4 * n : 4 * n + 3], dst.at[2 + 3 * n : 5 + 3 * n])
        for src, dst in ((x0s, x0b), (ys, yb), (ks, kb), (vs, vb))
        for n in range(2)
    ]
    copies = start_copies(
        [
            (own_hbm.at[0:2], own.at[0:2]), (own_hbm.at[29:32], own.at[2:5]), (wconv_hbm, wconv),
            (wqkv_hbm.at[0], wqkv), (table_hbm, table), (wout_hbm.at[0], wout),
        ]
        + held,
        sems,
    )
    top = jnp.where(pos[0] == 0, 0.0, 1.0).astype(BF16)
    mask = rim_mask(pos)
    extra = near_inside(pos, krow, kcol)
    copies[0].wait()
    copies[1].wait()

    def main(e):
        if e < 7:
            row = up[e][:64]
            return row * top if e == 6 else row
        if e >= 39:
            return down[e - 39][:64]
        return own[e - 7] if e < 9 else own[e - 7 - 27]

    def rim(e):
        if 7 <= e < 39:
            return jnp.concatenate([left[e - 7], right[e - 7]], axis=0) * mask
        row = (up[e] if e < 7 else down[e - 39])[64:] * mask
        return row * top if e == 6 else row

    conv_taps(cat, pick, (0, 1, 9, 10), main, rim)
    copies[2].wait()
    copies[3].wait()
    made = tokens_of(cat[...], wconv, wqkv, bconv, gain0, shift0, gains, shifts, bqkv)
    for ref, t in zip((x0b, yb, kb, vb), made):
        ref[0:2] = t[:2]
        ref[8:10] = t[2:]
    for copy in copies[4:]:
        copy.wait()
    outer = near_rows(
        (0, 5), (0, 1, 6, 7), x0b, yb, kb, vb, qsel, table, extra, wqkv, wout, bqkv, bout
    )
    mid = x1mid[...]
    for half, src in enumerate(
        (jnp.concatenate([outer[:128], mid[128:]], axis=0), jnp.concatenate([mid[:128], outer[128:]], axis=0))
    ):
        out[256 * half : 256 * half + 256] = jnp.dot(
            send[half], src, preferred_element_type=F32
        ).astype(BF16)


def far_first(
    pos, wqkv_hbm, wout_hbm, got, gains, shifts, bqkv, ksel, table, bout, ka, va, qs, ends, done, ys, yk,
    wqkv, wout, sems,
):
    copies = start_copies(((wqkv_hbm.at[1], wqkv), (wout_hbm.at[1], wout)), sems)
    ys[...] = norm(got[...].astype(F32), gains[1:2], shifts[1:2]).astype(BF16)
    for j in range(7):
        yk[64 * j : 64 * j + 64] = jnp.dot(
            ksel[...], ys[64 * j : 64 * j + 128], preferred_element_type=F32
        ).astype(BF16)
    ends[0:64] = ys[0:64]
    ends[64:128] = ys[448:512]
    copies[0].wait()
    kv = project(yk[...], wqkv[:, C3:], bqkv[1:2, C3:])
    ka[...] = kv[:, :C3].astype(BF16)
    va[...] = kv[:, C3:].astype(BF16)
    q = scaled(project(ys[...], wqkv[:, :C3], bqkv[1:2, :C3]))
    qs[0:128] = q[0:128]
    qs[128:256] = q[384:512]
    outs = []
    for m in range(2, 6):
        keys = slice(64 * (m - 2), 64 * (m - 2) + 256)
        outs.append(attend_block(q[64 * m : 64 * m + 64], ka[keys], va[keys], lambda g: table[g], None))
    copies[1].wait()
    x2 = project(jnp.concatenate(outs, axis=0), wout[...], bout[1:2])
    done[...] = (x2 + got[128:384].astype(F32)).astype(BF16)


def far_second(
    pos, wqkv_hbm, wout_hbm, above, below, got, ka, va, qs, ends, done, gains, shifts, bqkv, ksel, table,
    bout, out, yk, wkv, wout, sems,
):
    copies = start_copies(((wqkv_hbm.at[1, :, C3:], wkv), (wout_hbm.at[1], wout)), sems)
    zi, zsize = pos[2], pos[5]
    out[128:384] = done[...]

    def y_of(ref):
        return norm(ref[...].astype(F32), gains[1:2], shifts[1:2]).astype(BF16)

    over = jnp.concatenate([y_of(above), ends[0:64]], axis=0)
    under = jnp.concatenate([ends[64:128], y_of(below)], axis=0)
    for j in range(4):
        rows = (over if j < 2 else under)[64 * (j % 2) : 64 * (j % 2) + 128]
        yk[64 * j : 64 * j + 64] = jnp.dot(ksel[...], rows, preferred_element_type=F32).astype(BF16)
    copies[0].wait()
    kv = project(yk[...], wkv[...], bqkv[1:2, C3:]).astype(BF16)
    key_row = lax.broadcasted_iota(jnp.int32, (1, 256), 1) // 32 - 3
    outs = []
    for i, m in enumerate((0, 1, 6, 7)):
        row = key_row + (16 * zi + 2 * m)
        extra = jnp.where((row >= 0) & (row < 16 * zsize), 0.0, NEG)

        def keys(fresh, held):
            parts = (
                [fresh[0:128], held[0:128]], [fresh[64:128], held[0:192]],
                [held[256:448], fresh[128:192]], [held[320:448], fresh[128:256]],
            )[i]
            return jnp.concatenate(parts, axis=0)

        k, v = keys(kv[:, :C3], ka), keys(kv[:, C3:], va)
        outs.append(attend_block(qs[64 * i : 64 * i + 64], k, v, lambda g: table[g], extra))
    copies[1].wait()
    x2 = project(jnp.concatenate(outs, axis=0), wout[...], bout[1:2])
    out[0:128] = (x2[0:128] + got[0:128].astype(F32)).astype(BF16)
    out[384:512] = (x2[128:256] + got[384:512].astype(F32)).astype(BF16)


def back_kernel(got, sel, out):
    for i in range(8):
        rows = jnp.dot(sel[...], got[64 * i : 64 * i + 64], preferred_element_type=F32).astype(BF16)
        out[i] = rows[:32]
        out[8 + i] = rows[32:]


def call(kernel, out_shapes, scratch, args, smem=0, hbm=0, sems=0, flops=0, vmem=VMEM_NEAR):
    specs = [pl.BlockSpec(memory_space=pltpu.SMEM)] * smem
    specs += [pl.BlockSpec(memory_space=pltpu.HBM)] * hbm
    specs += [pl.BlockSpec(memory_space=pltpu.VMEM)] * (len(args) - smem - hbm)
    shapes = [pltpu.VMEM(s, t) for s, t in scratch]
    if sems:
        shapes.append(pltpu.SemaphoreType.DMA((sems,)))
    return pl.pallas_call(
        kernel,
        out_shape=[jax.ShapeDtypeStruct(s, t) for s, t in out_shapes],
        in_specs=specs,
        out_specs=[pl.BlockSpec(memory_space=pltpu.VMEM)] * len(out_shapes),
        scratch_shapes=shapes,
        compiler_params=pltpu.CompilerParams(vmem_limit_bytes=vmem * 2**20),
        cost_estimate=pl.CostEstimate(flops=flops, bytes_accessed=4 * 2**20, transcendentals=0),
    )(*args)


def build_tables(rel):
    hot0, code0 = near_patterns()
    hot1, code1 = far_patterns()
    return call(
        table_kernel,
        [((2, 2, GROUP * 64, 256), F32), ((2, GROUP * 64, 256), F32)],
        [],
        [rel, bf(hot0), jnp.asarray(code0), bf(hot1), jnp.asarray(code1)],
        flops=3 * 10**9, vmem=VMEM_TABLE,
    )


def near_consts():
    krow, kcol = near_keys()
    rows = np.repeat(np.arange(4) * 4, 2)[:, None] + np.tile(krow, (4, 1)) - 3
    cols = np.tile(np.arange(2) * 16, 4)[:, None] + np.tile(kcol, (4, 1)) - 3
    return [jnp.asarray(rows), jnp.asarray(cols), bf(query_matrix())]


def tall(n):
    return ((n, C3), BF16)


INNER = ((7, PT, C3), BF16)
WEIGHTS = [((9 * C2, C3), BF16), ((C3, 3 * C3), BF16)]
NEAR_COPIES = WEIGHTS + [tall(C3), ((2, 2, GROUP * 64, 256), F32)]


def near_first_call(pos, fmap, wconv, wqkv, wout, table, left, right, vecs):
    return call(
        near_first,
        [INNER, INNER, INNER, INNER, tall(256)],
        [((7 * PT, 9 * C2), BF16), ((32, 64, C2), BF16)] + NEAR_COPIES,
        [
            pos, fmap, wconv, wqkv, wout, table, left, right, bf(pick_matrix()), *vecs, *near_consts(),
        ],
        smem=1, hbm=5, sems=5, flops=8 * 10**9,
    )


def near_second_call(pos, fmap, wconv, wqkv, wout, table, up, down, left, right, first, vecs):
    part = ((10, PT, C3), BF16)
    (x1,) = call(
        near_second,
        [tall(512)],
        [((4 * PT, 9 * C2), BF16), part, part, part, part, ((5, 64, C2), BF16)] + NEAR_COPIES,
        [
            pos, fmap, wconv, wqkv, wout, table, up, down, left, right, *first, bf(pick_matrix()), *vecs,
            *near_consts(), bf(send_matrix()),
        ],
        smem=1, hbm=5, sems=14, flops=6 * 10**9,
    )
    return x1


def far_first_call(pos, wqkv, wout, got, gains, shifts, bqkv, table, bout):
    return call(
        far_first,
        [tall(448), tall(448), tall(256), tall(128), tall(256)],
        [tall(512), tall(448), WEIGHTS[1], tall(C3)],
        [pos, wqkv, wout, got, gains, shifts, bqkv, bf(far_key_matrix()), table, bout],
        smem=1, hbm=2, sems=2, flops=6 * 10**9, vmem=VMEM_FAR,
    )


def far_second_call(pos, wqkv, wout, above, below, got, first, gains, shifts, bqkv, table, bout):
    (x2,) = call(
        far_second,
        [tall(512)],
        [tall(256), ((C3, 2 * C3), BF16), tall(C3)],
        [
            pos, wqkv, wout, above, below, got, *first, gains, shifts, bqkv, bf(far_key_matrix()), table, bout,
        ],
        smem=1, hbm=2, sems=2, flops=4 * 10**9, vmem=VMEM_FAR,
    )
    return x2


def per_device(
    zsize, isize, xsize,
    fmap, wconv, bconv, gain0, shift0, gains, shifts, wqkv, bqkv, rel, wout, bout,
):
    zi, ii, xi = lax.axis_index("gz"), lax.axis_index("gi"), lax.axis_index("gx")
    ysize = zsize * isize
    yi = zi * isize + ii
    pos = jnp.stack([yi, xi, zi, ysize, xsize, zsize]).astype(jnp.int32)

    def shifted(x, dy, dx):
        pairs = [
            (y * xsize + c, ((y + dy) % ysize) * xsize + (c + dx) % xsize)
            for y in range(ysize)
            for c in range(xsize)
        ]
        return lax.ppermute(x, ("gz", "gi", "gx"), pairs)

    row = lambda v: v.reshape(1, C3)
    left, right = shifted(fmap[:, 56:], 0, 1), shifted(fmap[:, :8], 0, -1)
    table0, table1 = build_tables(rel)
    wconv = wconv.reshape(9 * C2, C3)
    vecs = [row(bconv), row(gain0), row(shift0), gains, shifts, bqkv, bout]

    def strip(at):
        return jnp.concatenate([fmap[at], left[at], right[at]], axis=1)

    up, down = shifted(strip(slice(25, 32)), 1, 0), shifted(strip(slice(0, 6)), -1, 0)
    first = near_first_call(pos, fmap, wconv, wqkv, wout, table0, left, right, vecs)
    x1 = near_second_call(pos, fmap, wconv, wqkv, wout, table0, up, down, left, right, first, vecs)
    got = lax.all_to_all(x1.reshape(64, 8, C3), ("gi", "gx"), 0, 0).reshape(512, C3)
    above = shifted(got[384:], isize, 0)
    below = shifted(got[:128], -isize, 0)
    first = far_first_call(pos, wqkv, wout, got, gains, shifts, bqkv, table1, bout)
    x2 = far_second_call(pos, wqkv, wout, above, below, got, first, gains, shifts, bqkv, table1, bout)
    back = lax.all_to_all(x2.reshape(64, 8, C3), ("gi", "gx"), 0, 0).reshape(512, C3)
    (out,) = call(back_kernel, [((TR, TC, C3), BF16)], [], [back, bf(back_matrix())], flops=10**8, vmem=VMEM_BACK)
    return out


def solution(mesh):
    gy, gx = mesh.shape["gy"], mesh.shape["gx"]
    inner = Mesh(mesh.devices.reshape(gy // 8, 8, gx), ("gz", "gi", "gx"))
    tile = P(("gz", "gi"), "gx", None)
    placed = (tile,) + (P(),) * 11
    return jax.shard_map(
        functools.partial(per_device, gy // 8, 8, gx),
        mesh=inner,
        in_specs=placed,
        out_specs=tile,
        check_vma=False,
    )
```

time: 101 us -> 90.7 us (0.90)
  waiting for transfers between devices: 15 us -> 3.67 us
  Pallas kernels: 24 us -> 29.4 us
  blocking collectives: 48.6 us -> 45.5 us
  local copies, waits for them, and re-layouts: 3.2 us -> 1.22 us
    ppermute x6, waiting for transfers between devices: 15 us -> 3.67 us  [shifted(): return lax.ppermute(x, ('gz', 'gi', 'gx'), pairs)]
    pallas_call x4 -> x6, Pallas kernels: 24 us -> 29.4 us  [call(): pl.pallas_call(kernel, out_shape=[jax.ShapeDtypeStruct(s, t) for s, t in...]
    all_to_all x1, blocking collectives: 30.8 us -> 27.6 us  [per_device(): lax.all_to_all(x1.reshape(64, 8, C3), ('gi', 'gx'), 0, 0).reshape(512, C3)]
    slice x5 -> x9, local copies, waits for them, and re-layouts: 2.96 us -> 1.01 us  [the longest x1 0.99 us: per_device(): left, right = (shifted(fmap[:, 56:], 0, 1), shifted(fmap[:, :8], 0, -1))]
  transfers between devices with their start and end apart: 6 -> 6, of which waited for: 6 -> 2; matrix products, arithmetic and copies ran while one was open for 2% -> 0% of each run, Pallas kernels for 2% -> 18%
where the time goes in v2:
time: 90.7 us; the launch traced here: 90.5 us
  blocking collectives  45.5 us (50%)
  Pallas kernels  29.4 us (32%)
  starting transfers between devices  10.3 us (11%)
  waiting for transfers between devices  3.67 us (4%)
  local copies, waits for them, and re-layouts  1.22 us (1%)
    pallas_call x6, Pallas kernels, call(): pl.pallas_call(kernel, out_shape=[jax.ShapeDtypeStruct(s, t) for s, t in...  29.4 us
    all_to_all x1, blocking collectives, per_device(): lax.all_to_all(x1.reshape(64, 8, C3), ('gi', 'gx'), 0, 0).reshape(512, C3)  27.6 us
    all_to_all x1, blocking collectives, per_device(): lax.all_to_all(x2.reshape(64, 8, C3), ('gi', 'gx'), 0, 0).reshape(512, C3)  17.9 us
    ppermute x6, starting transfers between devices, shifted(): return lax.ppermute(x, ('gz', 'gi', 'gx'), pairs)  10.3 us
    ppermute x6, waiting for transfers between devices, shifted(): return lax.ppermute(x, ('gz', 'gi', 'gx'), pairs)  3.67 us
  transfers between devices with their start and end apart: 6, of which 2 were waited for; matrix products, arithmetic and copies ran while one was open for 0% of the time, Pallas kernels for 18%

profile of v2, /device:TPU:1, one launch (start us, length us, event | category | flops | bytes accessed | tf_op | source)
XLA Modules:
  0.0 90.5 jit_solution(9789756536545345169)
XLA Ops:
  0.0 1.0 %fusion = (bf16[32,8,256]{2,1,0:T(8,128)(2,1)S(1)}, bf16[32,8,256]{2,1,0:T(8,128)(2,1)S(1)}) fusion(bf16[32,64,256]{2,1,0:T(8,128)(2,1)} %own_hbm.3), kind=kLoop, calls=%fused_computation.4 | loop fusion | bytes 524288 | tf_op jit(solution)/shard_map/slice | solution.py:562
  1.0 2.5 %collective-permute-start = (bf16[32,8,256]{2,1,0:T(8,128)(2,1)S(1)}, bf16[32,8,256]{2,1,0:T(8,128)(2,1)S(1)}, u32[]{:S(2)}, u32[]{:S(2)}) collective-permute-start(bf16[32,8,256]{2,1,0:T(8,128)(2,1)S(1)} %get-tuple-element.29), channel_id=1, source_target_pairs={{0,1},{1,2},{2,3},{3,4},{4,5},{5,6},{6,7},{7,0},{8,9},{9,10},{10,1... | collective-permute-start | bytes 393224 | tf_op jit(solution)/shard_map/ppermute | solution.py:559
  3.5 0.0 copy-start.5
  3.6 0.0 copy-start.6
  3.6 0.0 copy-start.7
  3.6 0.0 copy-start.8
  3.6 0.0 copy-start.9
  3.6 0.0 copy-start.10
  3.6 0.0 copy-start.11
  3.6 0.0 copy-start.13
  3.6 0.0 copy-start.14
  3.7 0.0 copy-start.16
  3.7 0.0 copy-start.17
  3.7 2.3 %collective-permute-start.1 = (bf16[32,8,256]{2,1,0:T(8,128)(2,1)S(1)}, bf16[32,8,256]{2,1,0:T(8,128)(2,1)S(1)}, u32[]{:S(2)}, u32[]{:S(2)}) collective-permute-start(bf16[32,8,256]{2,1,0:T(8,128)(2,1)S(1)} %get-tuple-element.30), channel_id=1, source_target_pairs={{0,7},{1,0},{2,1},{3,2},{4,3},{5,4},{6,5},{7,6},{8,15},{9,8},{10,9... | collective-permute-start | bytes 393224 | tf_op jit(solution)/shard_map/ppermute | solution.py:559
  6.0 4.4 %shard_map.262 = (f32[2,2,512,256]{3,2,1,0:T(8,128)}, f32[2,512,256]{2,1,0:T(8,128)}) custom-call(f32[2,16,49]{2,1,0:T(8,128)} %rel.1, bf16[49,4096]{1,0:T(8,128)(2,1)} %constant.42.clone.hot0, s32[2,64,256]{2,1,0:T(8,128)} %constant.43.clone.code0, bf16[49,512]{1,0:T(8,128)(2,1)} %constant.44.clone.hot1, s32[64,256]{1,0:T(8,128)} %constant.45.clone.code1), custom_call_target="tpu_custom_call" | custom-call | flops 3000000000 | bytes 4194304 | tf_op jit(solution)/shard_map/pallas_call | solution.py:455
  10.4 0.1 stack.15.pos
  10.5 2.7 %collective-permute-start.3 = (bf16[6,80,256]{2,1,0:T(8,128)(2,1)S(1)}, bf16[6,80,256]{2,1,0:T(8,128)(2,1)S(1)}, u32[]{:S(2)}, u32[]{:S(2)}) collective-permute-start(bf16[6,80,256]{2,1,0:T(8,128)(2,1)S(1)} %pad_maximum_fusion.1), channel_id=1, source_target_pairs={{0,248},{1,249},{2,250},{3,251},{4,252},{5,253},{6,254},{7,255},{8... | collective-permute-start | bytes 737288 | tf_op jit(solution)/shard_map/ppermute | solution.py:559
  13.3 0.3 collective-permute-start.2
  13.7 0.0 copy-start.12
  13.7 7.8 %shard_map.263 = (bf16[7,80,512]{2,1,0:T(8,128)(2,1)S(1)}, bf16[7,80,512]{2,1,0:T(8,128)(2,1)S(1)}, bf16[7,80,512]{2,1,0:T(8,128)(2,1)S(1)}, bf16[7,80,512]{2,1,0:T(8,128)(2,1)S(1)}, bf16[256,512]{1,0:T(8,128)(2,1)S(1)}) custom-call(s32[6]{0:T(128)S(1)} %stack.15.pos, bf16[32,64,256]{2,1,0:T(8,128)(2,1)S(1)} %copy-done, bf16[2304,512]{1,0:T(8,128)(2,1)} %bitcast.26, ...), custom_call_target="tpu_custom_call" | custom-call | flops 8000000000 | bytes 4194304 | tf_op jit(solution)/shard_map/pallas_call | solution.py:455
  21.6 0.0 copy-start.2
  21.6 0.0 copy-start.15
  21.6 8.6 %shard_map.264 = bf16[512,512]{1,0:T(8,128)(2,1)S(1)} custom-call(s32[6]{0:T(128)S(1)} %stack.15.pos, bf16[32,64,256]{2,1,0:T(8,128)(2,1)S(1)} %copy-done, bf16[2304,512]{1,0:T(8,128)(2,1)} %bitcast.27, bf16[2,512,1536]{2,1,0:T(8,128)(2,1)} %wqkv_hbm.7, bf16[2,512,512]{2,1,0:T(8,128)(2,1)} %wout_hbm.7, f32[2,2,512,256]{3,2,1,0:T(8,128)} %get-tuple-element.17.table_hbm, ...), custom_call_target="tpu_custom_call" | custom-call | flops 6000000000 | bytes 4194304 | tf_op jit(solution)/shard_map/pallas_call | solution.py:455
  30.2 27.6 %all_to_all.10 = bf16[64,8,512]{2,1,0:T(8,128)(2,1)S(1)} all-to-all(bf16[64,8,512]{2,1,0:T(8,128)(2,1)S(1)} %bitcast.18), channel_id=1, replica_groups=mesh['gz'=4,'gi'=8,'gx'=8] {'gi','gx'}, dimensions={0} | all-to-all | bytes 1048576 | tf_op jit(solution)/shard_map/all_to_all | solution.py:573
  57.8 1.3 %collective-permute-start.5 = (bf16[128,512]{1,0:T(8,128)(2,1)S(1)}, bf16[128,512]{1,0:T(8,128)(2,1)S(1)}, u32[]{:S(2)}, u32[]{:S(2)}) collective-permute-start(bf16[128,512]{1,0:T(8,128)(2,1)S(1)} %get-tuple-element.31), channel_id=1, source_target_pairs={{0,192},{1,193},{2,194},{3,195},{4,196},{5,197},{6,198},{7,199},{8... | collective-permute-start | bytes 393224 | tf_op jit(solution)/shard_map/ppermute | solution.py:559
  59.1 1.2 %collective-permute-start.4 = (bf16[128,512]{1,0:T(8,128)(2,1)S(1)}, bf16[128,512]{1,0:T(8,128)(2,1)S(1)}, u32[]{:S(2)}, u32[]{:S(2)}) collective-permute-start(bf16[128,512]{1,0:T(8,128)(2,1)S(1)} %get-tuple-element.32), channel_id=1, source_target_pairs={{0,64},{1,65},{2,66},{3,67},{4,68},{5,69},{6,70},{7,71},{8,72},{9,... | collective-permute-start | bytes 393224 | tf_op jit(solution)/shard_map/ppermute | solution.py:559
  60.3 4.1 %shard_map.265 = (bf16[448,512]{1,0:T(8,128)(2,1)S(1)}, bf16[448,512]{1,0:T(8,128)(2,1)S(1)}, bf16[256,512]{1,0:T(8,128)(2,1)S(1)}, bf16[128,512]{1,0:T(8,128)(2,1)S(1)}, bf16[256,512]{1,0:T(8,128)(2,1)S(1)}) custom-call(s32[6]{0:T(128)S(1)} %stack.15.pos, bf16[2,512,1536]{2,1,0:T(8,128)(2,1)S(1)} %copy-done.2, bf16[2,512,512]{2,1,0:T(8,128)(2,1)S(1)} %copy-done.4, ...), custom_call_target="tpu_custom_call" | custom-call | flops 6000000000 | bytes 4194304 | tf_op jit(solution)/shard_map/pallas_call | solution.py:455
  64.4 2.4 %collective-permute-done.5.below = bf16[128,512]{1,0:T(8,128)(2,1)S(1)} collective-permute-done((bf16[128,512]{1,0:T(8,128)(2,1)S(1)}, bf16[128,512]{1,0:T(8,128)(2,1)S(1)}, u32[]{:S(2)}, u32[]{:S(2)}) %collective-permute-start.5) | collective-permute-done | bytes 131104 | tf_op jit(solution)/shard_map/ppermute | solution.py:559
  66.8 1.3 %collective-permute-done.4.above = bf16[128,512]{1,0:T(8,128)(2,1)S(1)} collective-permute-done((bf16[128,512]{1,0:T(8,128)(2,1)S(1)}, bf16[128,512]{1,0:T(8,128)(2,1)S(1)}, u32[]{:S(2)}, u32[]{:S(2)}) %collective-permute-start.4) | collective-permute-done | bytes 131104 | tf_op jit(solution)/shard_map/ppermute | solution.py:559
  68.0 3.5 %shard_map.266 = bf16[512,512]{1,0:T(8,128)(2,1)S(1)} custom-call(s32[6]{0:T(128)S(1)} %stack.15.pos, bf16[2,512,1536]{2,1,0:T(8,128)(2,1)S(1)} %copy-done.2, bf16[2,512,512]{2,1,0:T(8,128)(2,1)S(1)} %copy-done.4, bf16[128,512]{1,0:T(8,128)(2,1)S(1)} %collective-permute-done.4.above, bf16[128,512]{1,0:T(8,128)(2,1)S(1)} %collective-permute-done.5.below, ...), custom_call_target="tpu_custom_call" | custom-call | flops 4000000000 | bytes 4194304 | tf_op jit(solution)/shard_map/pallas_call | solution.py:455
  71.5 17.9 %all_to_all.11 = bf16[64,8,512]{2,1,0:T(8,128)(2,1)S(1)} all-to-all(bf16[64,8,512]{2,1,0:T(8,128)(2,1)S(1)} %bitcast.19), channel_id=1, replica_groups=mesh['gz'=4,'gi'=8,'gx'=8] {'gi','gx'}, dimensions={0} | all-to-all | bytes 1048576 | tf_op jit(solution)/shard_map/all_to_all | solution.py:578
  89.4 1.1 %shard_map.267 = bf16[16,32,512]{2,1,0:T(8,128)(2,1)} custom-call(bf16[512,512]{1,0:T(8,128)(2,1)S(1)} %bitcast.15, bf16[64,64]{1,0:T(8,128)(2,1)S(1)} %copy-done.1), custom_call_target="tpu_custom_call" | custom-call | flops 100000000 | bytes 4194304 | tf_op jit(solution)/shard_map/pallas_call | solution.py:455
  (39 shorter events, 0.1 us)
Async XLA Ops:
  1.0 9.5 %collective-permute-start = (bf16[32,8,256]{2,1,0:T(8,128)(2,1)S(1)}, bf16[32,8,256]{2,1,0:T(8,128)(2,1)S(1)}, u32[]{:S(2)}, u32[]{:S(2)}) collective-permute-start(bf16[32,8,256]{2,1,0:T(8,128)(2,1)S(1)} %get-tuple-element.29), channel_id=1, source_target_pairs={{0,1},{1,2},{2,3},{3,4},{4,5},{5,6},{6,7},{7,0},{8,9},{9,10},{10,1... | collective-permute-start | bytes 393224 | tf_op jit(solution)/shard_map/ppermute | solution.py:559
  3.5 7.0 %slice-start = ((bf16[32,64,256]{2,1,0:T(8,128)(2,1)}), bf16[6,64,256]{2,1,0:T(8,128)(2,1)S(1)}, s32[]{:S(2)}) async-start(bf16[32,64,256]{2,1,0:T(8,128)(2,1)} %own_hbm.3), calls=%async_computation.2 | async-start | bytes 393216 | tf_op jit(solution)/shard_map/slice | solution.py:568
  3.5 9.8 %slice-start.1 = ((bf16[32,64,256]{2,1,0:T(8,128)(2,1)}), bf16[7,64,256]{2,1,0:T(8,128)(2,1)S(1)}, s32[]{:S(2)}) async-start(bf16[32,64,256]{2,1,0:T(8,128)(2,1)} %own_hbm.3), calls=%async_computation.3 | async-start | bytes 458752 | tf_op jit(solution)/shard_map/slice | solution.py:568
  3.5 10.1 %copy-start = (bf16[32,64,256]{2,1,0:T(8,128)(2,1)S(1)}, bf16[32,64,256]{2,1,0:T(8,128)(2,1)}, u32[]{:S(2)}) copy-start(bf16[32,64,256]{2,1,0:T(8,128)(2,1)} %own_hbm.3) | copy-start | bytes 3145732
  3.5 10.1 %copy-start.3 = (bf16[2,512,512]{2,1,0:T(8,128)(2,1)S(1)}, bf16[2,512,512]{2,1,0:T(8,128)(2,1)}, u32[]{:S(2)}) copy-start(bf16[2,512,512]{2,1,0:T(8,128)(2,1)} %wout_hbm.7) | copy-start | bytes 3145732
  3.5 10.1 %copy-start.5 = (f32[2,1536]{1,0:T(2,128)S(1)}, f32[2,1536]{1,0:T(2,128)}, u32[]{:S(2)}) copy-start(f32[2,1536]{1,0:T(2,128)} %bqkv.7) | copy-start | bytes 36868
  3.6 10.1 %copy-start.6 = (f32[2,512]{1,0:T(2,128)S(1)}, f32[2,512]{1,0:T(2,128)}, u32[]{:S(2)}) copy-start(f32[2,512]{1,0:T(2,128)} %gains.7) | copy-start | bytes 12292
  3.6 10.1 %copy-start.7 = (f32[2,512]{1,0:T(2,128)S(1)}, f32[2,512]{1,0:T(2,128)}, u32[]{:S(2)}) copy-start(f32[2,512]{1,0:T(2,128)} %shifts.7) | copy-start | bytes 12292
  3.6 10.1 %copy-start.8 = (f32[2,512]{1,0:T(2,128)S(1)}, f32[2,512]{1,0:T(2,128)}, u32[]{:S(2)}) copy-start(f32[2,512]{1,0:T(2,128)} %bout.7) | copy-start | bytes 12292
  3.6 10.1 %copy-start.9 = (f32[512]{0:T(512)S(1)}, f32[512]{0:T(512)}, u32[]{:S(2)}) copy-start(f32[512]{0:T(512)} %param.30) | copy-start | bytes 6148
  3.6 10.1 %copy-start.10 = (f32[512]{0:T(512)S(1)}, f32[512]{0:T(512)}, u32[]{:S(2)}) copy-start(f32[512]{0:T(512)} %param.31) | copy-start | bytes 6148
  3.6 10.1 %copy-start.11 = (f32[512]{0:T(512)S(1)}, f32[512]{0:T(512)}, u32[]{:S(2)}) copy-start(f32[512]{0:T(512)} %param.32) | copy-start | bytes 6148
  3.6 10.1 %copy-start.13 = (bf16[240,160]{1,0:T(8,128)(2,1)S(1)}, bf16[240,160]{1,0:T(8,128)(2,1)}, u32[]{:S(2)}) copy-start(bf16[240,160]{1,0:T(8,128)(2,1)} %constant.46.clone.pick) | copy-start | bytes 230404
  3.6 10.1 %copy-start.14 = (bf16[2,64,256]{2,1,0:T(8,128)(2,1)S(1)}, bf16[2,64,256]{2,1,0:T(8,128)(2,1)}, u32[]{:S(2)}) copy-start(bf16[2,64,256]{2,1,0:T(8,128)(2,1)} %constant.49.clone.qsel) | copy-start | bytes 196612
  3.7 10.1 %copy-start.16 = (s32[8,256]{1,0:T(8,128)S(1)}, s32[8,256]{1,0:T(8,128)}, u32[]{:S(2)}) copy-start(s32[8,256]{1,0:T(8,128)} %constant.48.clone.kcol) | copy-start | bytes 24580
  3.7 10.1 %copy-start.17 = (s32[8,256]{1,0:T(8,128)S(1)}, s32[8,256]{1,0:T(8,128)}, u32[]{:S(2)}) copy-start(s32[8,256]{1,0:T(8,128)} %constant.47.clone.krow) | copy-start | bytes 24580
  3.7 6.8 %collective-permute-start.1 = (bf16[32,8,256]{2,1,0:T(8,128)(2,1)S(1)}, bf16[32,8,256]{2,1,0:T(8,128)(2,1)S(1)}, u32[]{:S(2)}, u32[]{:S(2)}) collective-permute-start(bf16[32,8,256]{2,1,0:T(8,128)(2,1)S(1)} %get-tuple-element.30), channel_id=1, source_target_pairs={{0,7},{1,0},{2,1},{3,2},{4,3},{5,4},{6,5},{7,6},{8,15},{9,8},{10,9... | collective-permute-start | bytes 393224 | tf_op jit(solution)/shard_map/ppermute | solution.py:559
  10.5 11.0 %collective-permute-start.3 = (bf16[6,80,256]{2,1,0:T(8,128)(2,1)S(1)}, bf16[6,80,256]{2,1,0:T(8,128)(2,1)S(1)}, u32[]{:S(2)}, u32[]{:S(2)}) collective-permute-start(bf16[6,80,256]{2,1,0:T(8,128)(2,1)S(1)} %pad_maximum_fusion.1), channel_id=1, source_target_pairs={{0,248},{1,249},{2,250},{3,251},{4,252},{5,253},{6,254},{7,255},{8... | collective-permute-start | bytes 737288 | tf_op jit(solution)/shard_map/ppermute | solution.py:559
  13.3 8.2 %collective-permute-start.2 = (bf16[7,80,256]{2,1,0:T(8,128)(2,1)S(1)}, bf16[7,80,256]{2,1,0:T(8,128)(2,1)S(1)}, u32[]{:S(2)}, u32[]{:S(2)}) collective-permute-start(bf16[7,80,256]{2,1,0:T(8,128)(2,1)S(1)} %pad_maximum_fusion), channel_id=1, source_target_pairs={{0,8},{1,9},{2,10},{3,11},{4,12},{5,13},{6,14},{7,15},{8,16},{9,17... | collective-permute-start | bytes 860168 | tf_op jit(solution)/shard_map/ppermute | solution.py:559
  13.7 7.8 %copy-start.12 = (bf16[2,256,256]{2,1,0:T(8,128)(2,1)S(1)}, bf16[2,256,256]{2,1,0:T(8,128)(2,1)}, u32[]{:S(2)}) copy-start(bf16[2,256,256]{2,1,0:T(8,128)(2,1)} %constant.50.clone.send) | copy-start | bytes 786436
  21.6 38.7 %copy-start.2 = (bf16[2,512,1536]{2,1,0:T(8,128)(2,1)S(1)}, bf16[2,512,1536]{2,1,0:T(8,128)(2,1)}, u32[]{:S(2)}) copy-start(bf16[2,512,1536]{2,1,0:T(8,128)(2,1)} %wqkv_hbm.7) | copy-start | bytes 9437188
  21.6 38.7 %copy-start.4 = (bf16[2,512,512]{2,1,0:T(8,128)(2,1)S(1)}, bf16[2,512,512]{2,1,0:T(8,128)(2,1)}, u32[]{:S(2)}) copy-start(bf16[2,512,512]{2,1,0:T(8,128)(2,1)} %wout_hbm.7) | copy-start | bytes 3145732
  21.6 38.7 %copy-start.15 = (bf16[64,128]{1,0:T(8,128)(2,1)S(1)}, bf16[64,128]{1,0:T(8,128)(2,1)}, u32[]{:S(2)}) copy-start(bf16[64,128]{1,0:T(8,128)(2,1)} %constant.51.clone.ksel) | copy-start | bytes 49156
  21.6 38.7 %copy-start.18 = (f32[2,512,256]{2,1,0:T(8,128)S(1)}, f32[2,512,256]{2,1,0:T(8,128)}, u32[]{:S(2)}) copy-start(f32[2,512,256]{2,1,0:T(8,128)} %get-tuple-element.23.table) | copy-start | bytes 3145732
  57.8 8.9 %collective-permute-start.5 = (bf16[128,512]{1,0:T(8,128)(2,1)S(1)}, bf16[128,512]{1,0:T(8,128)(2,1)S(1)}, u32[]{:S(2)}, u32[]{:S(2)}) collective-permute-start(bf16[128,512]{1,0:T(8,128)(2,1)S(1)} %get-tuple-element.31), channel_id=1, source_target_pairs={{0,192},{1,193},{2,194},{3,195},{4,196},{5,197},{6,198},{7,199},{8... | collective-permute-start | bytes 393224 | tf_op jit(solution)/shard_map/ppermute | solution.py:559
  59.1 9.0 %collective-permute-start.4 = (bf16[128,512]{1,0:T(8,128)(2,1)S(1)}, bf16[128,512]{1,0:T(8,128)(2,1)S(1)}, u32[]{:S(2)}, u32[]{:S(2)}) collective-permute-start(bf16[128,512]{1,0:T(8,128)(2,1)S(1)} %get-tuple-element.32), channel_id=1, source_target_pairs={{0,64},{1,65},{2,66},{3,67},{4,68},{5,69},{6,70},{7,71},{8,72},{9,... | collective-permute-start | bytes 393224 | tf_op jit(solution)/shard_map/ppermute | solution.py:559
  68.0 21.4 %copy-start.1 = (bf16[64,64]{1,0:T(8,128)(2,1)S(1)}, bf16[64,64]{1,0:T(8,128)(2,1)}, u32[]{:S(2)}) copy-start(bf16[64,64]{1,0:T(8,128)(2,1)} %constant.52.clone.sel) | copy-start | bytes 24580

commit v3 on v2

--- a/solution.py
+++ b/solution.py
@@ -24,7 +24,7 @@
 PT = 80
 NTOK = PAIRS * PT
 EPS = 1e-5
-VMEM_TABLE, VMEM_NEAR, VMEM_FAR, VMEM_BACK = 56, 48, 46, 46
+VMEM_TABLE, VMEM_NEAR, VMEM_FAR, VMEM_BACK = 56, 39, 46, 46
 
 
 def pair_slots():
@@ -254,36 +254,48 @@
     return jnp.concatenate([part, part[:16]], axis=0)
 
 
-def tokens_of(cat, wconv, wqkv, bconv, gain0, shift0, gains, shifts, bqkv):
+def outer_window(new, held, first, h):
+    at = slice(32 * h, 32 * h + 48)
+    parts = [new[0:2, at], held[0:3, at]] if first == 0 else [held[4:7, at], new[2:4, at]]
+    parts = [part.reshape(-1, C3) for part in parts]
+    return jnp.concatenate(parts + [parts[0][:16]], axis=0)
+
+
+def tokens_of(cat, wconv, wqkv, bconv, gain0, shift0, gains, shifts, bqkv, copy):
     x0 = norm(project(cat, wconv[...], bconv[...]), gain0[...], shift0[...]).astype(BF16)
     y = norm(x0.astype(F32), gains[0:1], shifts[0:1]).astype(BF16)
+    if copy is not None:
+        copy.wait()
     kv = project(y, wqkv[:, C3:], bqkv[0:1, C3:]).astype(BF16)
     return [t.reshape(-1, PT, C3) for t in (x0, y, kv[:, :C3], kv[:, C3:])]
 
 
-def near_rows(firsts, blocks, x0, y, k, v, qsel, table, extra, wqkv, wout, bqkv, bout):
+def near_rows(firsts, blocks, x0, y, k, v, qsel, table, extra, wqkv, wout, bqkv, bout, copies):
     yq, xq = [], []
     for first in firsts:
         for h in range(2):
-            yq.append(jnp.dot(qsel[h], window(y, first, h), preferred_element_type=F32).astype(BF16))
-            xq.append(jnp.dot(qsel[h], window(x0, first, h), preferred_element_type=F32))
+            yq.append(jnp.dot(qsel[h], y(first, h), preferred_element_type=F32).astype(BF16))
+            xq.append(jnp.dot(qsel[h], x0(first, h), preferred_element_type=F32))
     q = scaled(project(jnp.concatenate(yq, axis=0), wqkv[:, :C3], bqkv[0:1, :C3]))
     att = []
+    if len(copies) > 1:
+        copies[0].wait()
     for i, block in enumerate(blocks):
         first, h = firsts[i // 2], i % 2
         att.append(
             attend_block(
-                q[64 * i : 64 * i + 64], window(k, first, h), window(v, first, h), lambda g: table[h, g],
+                q[64 * i : 64 * i + 64], k(first, h), v(first, h), lambda g: table[h, g],
                 extra[block : block + 1],
             )
         )
+    copies[-1].wait()
     out = project(jnp.concatenate(att, axis=0), wout[...], bout[0:1]) + jnp.concatenate(xq, axis=0)
     return out.astype(BF16)
 
 
 def near_first(
     pos, own_hbm, wconv_hbm, wqkv_hbm, wout_hbm, table_hbm, left, right, pick, bconv, gain0, shift0, gains,
-    shifts, bqkv, bout, krow, kcol, qsel, x0s, ys, ks, vs, x1, cat, own, wconv, wqkv, wout, table, sems,
+    shifts, bqkv, bout, krow, kcol, qsel, x0s, ys, ks, vs, x1, wconv, wqkv, table, cat, own, wout, sems,
 ):
     copies = start_copies(
         (
@@ -301,33 +313,24 @@
 
     conv_taps(cat, pick, range(2, 9), lambda e: own[e - 7], rim)
     copies[1].wait()
-    copies[2].wait()
-    made = tokens_of(cat[...], wconv, wqkv, bconv, gain0, shift0, gains, shifts, bqkv)
+    made = tokens_of(cat[...], wconv, wqkv, bconv, gain0, shift0, gains, shifts, bqkv, copies[2])
     for ref, t in zip((x0s, ys, ks, vs), made):
         ref[...] = t
-    copies[3].wait()
-    copies[4].wait()
+    views = [functools.partial(window, ref) for ref in (x0s, ys, ks, vs)]
     x1[...] = near_rows(
-        (0, 2), (2, 3, 4, 5), x0s, ys, ks, vs, qsel, table, extra, wqkv, wout, bqkv, bout
+        (0, 2), (2, 3, 4, 5), *views, qsel, table, extra, wqkv, wout, bqkv, bout, copies[3:]
     )
 
 
 def near_second(
-    pos, own_hbm, wconv_hbm, wqkv_hbm, wout_hbm, table_hbm, up, down, left, right, x0s, ys, ks, vs, x1mid,
-    pick, bconv, gain0, shift0, gains, shifts, bqkv, bout, krow, kcol, qsel, send, out, cat, x0b, yb, kb, vb,
-    own, wconv, wqkv, wout, table, sems,
+    pos, own_hbm, wout_hbm, up, down, left, right, x0s, ys, ks, vs, x1mid, wconv, wqkv, table, pick, bconv,
+    gain0, shift0, gains, shifts, bqkv, bout, krow, kcol, qsel, send, out, cat, x0b, yb, kb, vb, own, wout,
+    sems,
 ):
-    held = [
-        (src.at[4 * n : 4 * n + 3], dst.at[2 + 3 * n : 5 + 3 * n])
-        for src, dst in ((x0s, x0b), (ys, yb), (ks, kb), (vs, vb))
-        for n in range(2)
-    ]
     copies = start_copies(
-        [
-            (own_hbm.at[0:2], own.at[0:2]), (own_hbm.at[29:32], own.at[2:5]), (wconv_hbm, wconv),
-            (wqkv_hbm.at[0], wqkv), (table_hbm, table), (wout_hbm.at[0], wout),
-        ]
-        + held,
+        (
+            (own_hbm.at[0:2], own.at[0:2]), (own_hbm.at[29:32], own.at[2:5]), (wout_hbm.at[0], wout),
+        ),
         sems,
     )
     top = jnp.where(pos[0] == 0, 0.0, 1.0).astype(BF16)
@@ -351,16 +354,15 @@
         return row * top if e == 6 else row
 
     conv_taps(cat, pick, (0, 1, 9, 10), main, rim)
-    copies[2].wait()
-    copies[3].wait()
-    made = tokens_of(cat[...], wconv, wqkv, bconv, gain0, shift0, gains, shifts, bqkv)
+    made = tokens_of(cat[...], wconv, wqkv, bconv, gain0, shift0, gains, shifts, bqkv, None)
     for ref, t in zip((x0b, yb, kb, vb), made):
-        ref[0:2] = t[:2]
-        ref[8:10] = t[2:]
-    for copy in copies[4:]:
-        copy.wait()
+        ref[...] = t
+    views = [
+        functools.partial(outer_window, new, held)
+        for new, held in ((x0b, x0s), (yb, ys), (kb, ks), (vb, vs))
+    ]
     outer = near_rows(
-        (0, 5), (0, 1, 6, 7), x0b, yb, kb, vb, qsel, table, extra, wqkv, wout, bqkv, bout
+        (0, 5), (0, 1, 6, 7), *views, qsel, table, extra, wqkv, wout, bqkv, bout, copies[2:]
     )
     mid = x1mid[...]
     for half, src in enumerate(
@@ -488,14 +490,14 @@
 
 INNER = ((7, PT, C3), BF16)
 WEIGHTS = [((9 * C2, C3), BF16), ((C3, 3 * C3), BF16)]
-NEAR_COPIES = WEIGHTS + [tall(C3), ((2, 2, GROUP * 64, 256), F32)]
+TABLE = ((2, 2, GROUP * 64, 256), F32)
 
 
 def near_first_call(pos, fmap, wconv, wqkv, wout, table, left, right, vecs):
     return call(
         near_first,
-        [INNER, INNER, INNER, INNER, tall(256)],
-        [((7 * PT, 9 * C2), BF16), ((32, 64, C2), BF16)] + NEAR_COPIES,
+        [INNER, INNER, INNER, INNER, tall(256), *WEIGHTS, TABLE],
+        [((7 * PT, 9 * C2), BF16), ((32, 64, C2), BF16), tall(C3)],
         [
             pos, fmap, wconv, wqkv, wout, table, left, right, bf(pick_matrix()), *vecs, *near_consts(),
         ],
@@ -503,17 +505,17 @@
     )
 
 
-def near_second_call(pos, fmap, wconv, wqkv, wout, table, up, down, left, right, first, vecs):
-    part = ((10, PT, C3), BF16)
+def near_second_call(pos, fmap, wout, up, down, left, right, first, vecs):
+    part = ((4, PT, C3), BF16)
     (x1,) = call(
         near_second,
         [tall(512)],
-        [((4 * PT, 9 * C2), BF16), part, part, part, part, ((5, 64, C2), BF16)] + NEAR_COPIES,
+        [((4 * PT, 9 * C2), BF16), part, part, part, part, ((5, 64, C2), BF16), tall(C3)],
         [
-            pos, fmap, wconv, wqkv, wout, table, up, down, left, right, *first, bf(pick_matrix()), *vecs,
+            pos, fmap, wout, up, down, left, right, *first, bf(pick_matrix()), *vecs,
             *near_consts(), bf(send_matrix()),
         ],
-        smem=1, hbm=5, sems=14, flops=6 * 10**9,
+        smem=1, hbm=2, sems=3, flops=6 * 10**9,
     )
     return x1
 
@@ -569,7 +571,7 @@
 
     up, down = shifted(strip(slice(25, 32)), 1, 0), shifted(strip(slice(0, 6)), -1, 0)
     first = near_first_call(pos, fmap, wconv, wqkv, wout, table0, left, right, vecs)
-    x1 = near_second_call(pos, fmap, wconv, wqkv, wout, table0, up, down, left, right, first, vecs)
+    x1 = near_second_call(pos, fmap, wout, up, down, left, right, first, vecs)
     got = lax.all_to_all(x1.reshape(64, 8, C3), ("gi", "gx"), 0, 0).reshape(512, C3)
     above = shifted(got[384:], isize, 0)
     below = shifted(got[:128], -isize, 0)

time: 90.7 us -> 86.8 us (0.957)
  local copies, waits for them, and re-layouts: 1.22 us -> 5.68 us
  blocking collectives: 45.5 us -> 41.4 us
  Pallas kernels: 29.4 us -> 25.9 us
  waiting for transfers between devices: 3.67 us -> 1.05 us
  starting transfers between devices: 10.3 us -> 12.1 us
    unnamed x38 -> x40, local copies, waits for them, and re-layouts: 0.11 us -> 4.58 us
    pallas_call x6, Pallas kernels: 29.4 us -> 25.9 us  [call(): pl.pallas_call(kernel, out_shape=[jax.ShapeDtypeStruct(s, t) for s, t in...]
    all_to_all x1, blocking collectives: 27.6 us -> 24.9 us  [per_device(): lax.all_to_all(x1.reshape(64, 8, C3), ('gi', 'gx'), 0, 0).reshape(512, C3)]
    ppermute x6, waiting for transfers between devices: 3.67 us -> 1.05 us  [shifted(): return lax.ppermute(x, ('gz', 'gi', 'gx'), pairs)]
    ppermute x6, starting transfers between devices: 10.3 us -> 12.1 us  [shifted(): return lax.ppermute(x, ('gz', 'gi', 'gx'), pairs)]
    all_to_all x1, blocking collectives: 17.9 us -> 16.5 us  [per_device(): lax.all_to_all(x2.reshape(64, 8, C3), ('gi', 'gx'), 0, 0).reshape(512, C3)]
where the time goes in v3:
time: 86.8 us; the launch traced here: 86.5 us
  blocking collectives  41.4 us (48%)
  Pallas kernels  25.9 us (30%)
  starting transfers between devices  12.1 us (14%)
  local copies, waits for them, and re-layouts  5.68 us (7%)
  waiting for transfers between devices  1.05 us (1%)
    pallas_call x6, Pallas kernels, call(): pl.pallas_call(kernel, out_shape=[jax.ShapeDtypeStruct(s, t) for s, t in...  25.9 us
    all_to_all x1, blocking collectives, per_device(): lax.all_to_all(x1.reshape(64, 8, C3), ('gi', 'gx'), 0, 0).reshape(512, C3)  24.9 us
    all_to_all x1, blocking collectives, per_device(): lax.all_to_all(x2.reshape(64, 8, C3), ('gi', 'gx'), 0, 0).reshape(512, C3)  16.5 us
    ppermute x6, starting transfers between devices, shifted(): return lax.ppermute(x, ('gz', 'gi', 'gx'), pairs)  12.1 us
    unnamed x40, local copies, waits for them, and re-layouts  4.58 us
  transfers between devices with their start and end apart: 6, of which 2 were waited for; matrix products, arithmetic and copies ran while one was open for 0% of the time, Pallas kernels for 18%

profile of v3, /device:TPU:1, one launch (start us, length us, event | category | flops | bytes accessed | tf_op | source)
XLA Modules:
  0.0 86.5 jit_solution(11271179094936833937)
XLA Ops:
  0.0 1.0 %fusion = (bf16[32,8,256]{2,1,0:T(8,128)(2,1)S(1)}, bf16[32,8,256]{2,1,0:T(8,128)(2,1)S(1)}) fusion(bf16[32,64,256]{2,1,0:T(8,128)(2,1)} %own_hbm.3), kind=kLoop, calls=%fused_computation.4 | loop fusion | bytes 524288 | tf_op jit(solution)/shard_map/slice | solution.py:564
  1.0 2.5 %collective-permute-start = (bf16[32,8,256]{2,1,0:T(8,128)(2,1)S(1)}, bf16[32,8,256]{2,1,0:T(8,128)(2,1)S(1)}, u32[]{:S(2)}, u32[]{:S(2)}) collective-permute-start(bf16[32,8,256]{2,1,0:T(8,128)(2,1)S(1)} %get-tuple-element.35), channel_id=1, source_target_pairs={{0,1},{1,2},{2,3},{3,4},{4,5},{5,6},{6,7},{7,0},{8,9},{9,10},{10,1... | collective-permute-start | bytes 393224 | tf_op jit(solution)/shard_map/ppermute | solution.py:561
  3.5 0.0 copy-start.5
  3.6 0.0 copy-start.6
  3.6 0.0 copy-start.7
  3.6 0.0 copy-start.8
  3.6 0.0 copy-start.9
  3.6 0.0 copy-start.13
  3.6 0.0 copy-start.14
  3.7 0.0 copy-start.16
  3.7 0.0 copy-start.17
  3.7 2.3 %collective-permute-start.1 = (bf16[32,8,256]{2,1,0:T(8,128)(2,1)S(1)}, bf16[32,8,256]{2,1,0:T(8,128)(2,1)S(1)}, u32[]{:S(2)}, u32[]{:S(2)}) collective-permute-start(bf16[32,8,256]{2,1,0:T(8,128)(2,1)S(1)} %get-tuple-element.36), channel_id=1, source_target_pairs={{0,7},{1,0},{2,1},{3,2},{4,3},{5,4},{6,5},{7,6},{8,15},{9,8},{10,9... | collective-permute-start | bytes 393224 | tf_op jit(solution)/shard_map/ppermute | solution.py:561
  6.0 4.4 %shard_map.262 = (f32[2,2,512,256]{3,2,1,0:T(8,128)}, f32[2,512,256]{2,1,0:T(8,128)}) custom-call(f32[2,16,49]{2,1,0:T(8,128)} %rel.1, bf16[49,4096]{1,0:T(8,128)(2,1)} %constant.42.clone.hot0, s32[2,64,256]{2,1,0:T(8,128)} %constant.43.clone.code0, bf16[49,512]{1,0:T(8,128)(2,1)} %constant.44.clone.hot1, s32[64,256]{1,0:T(8,128)} %constant.45.clone.code1), custom_call_target="tpu_custom_call" | custom-call | flops 3000000000 | bytes 4194304 | tf_op jit(solution)/shard_map/pallas_call | solution.py:457
  10.4 0.1 stack.15.pos
  10.5 2.7 %collective-permute-start.3 = (bf16[6,80,256]{2,1,0:T(8,128)(2,1)S(1)}, bf16[6,80,256]{2,1,0:T(8,128)(2,1)S(1)}, u32[]{:S(2)}, u32[]{:S(2)}) collective-permute-start(bf16[6,80,256]{2,1,0:T(8,128)(2,1)S(1)} %pad_maximum_fusion.1), channel_id=1, source_target_pairs={{0,248},{1,249},{2,250},{3,251},{4,252},{5,253},{6,254},{7,255},{8... | collective-permute-start | bytes 737288 | tf_op jit(solution)/shard_map/ppermute | solution.py:561
  13.3 0.3 collective-permute-start.2
  13.7 1.7 %copy-done.3 = bf16[3,3,256,512]{3,2,1,0:T(8,128)(2,1)S(1)} copy-done((bf16[3,3,256,512]{3,2,1,0:T(8,128)(2,1)S(1)}, bf16[3,3,256,512]{3,2,1,0:T(8,128)(2,1)}, u32[]{:S(2)}) %copy-start.3) | copy-done | bytes 2359320
  15.4 1.6 %copy-done.19 = f32[2,2,512,256]{3,2,1,0:T(8,128)S(1)} copy-done((f32[2,2,512,256]{3,2,1,0:T(8,128)S(1)}, f32[2,2,512,256]{3,2,1,0:T(8,128)}, u32[]{:S(2)}) %copy-start.19) | copy-done | bytes 2097176
  17.0 7.2 %shard_map.263 = (bf16[7,80,512]{2,1,0:T(8,128)(2,1)S(1)}, bf16[7,80,512]{2,1,0:T(8,128)(2,1)S(1)}, bf16[7,80,512]{2,1,0:T(8,128)(2,1)S(1)}, bf16[7,80,512]{2,1,...) custom-call(s32[6]{0:T(128)S(1)} %stack.15.pos, ...), custom_call_target="tpu_custom_call" | custom-call | flops 8000000000 | bytes 4194304 | tf_op jit(solution)/shard_map/pallas_call | solution.py:457
  24.2 0.0 copy-start.2
  24.3 0.0 copy-start.15
  24.3 5.6 %shard_map.264 = bf16[512,512]{1,0:T(8,128)(2,1)S(1)} custom-call(s32[6]{0:T(128)S(1)} %stack.15.pos, bf16[32,64,256]{2,1,0:T(8,128)(2,1)S(1)} %copy-done, bf16[2,512,512]{2,1,0:T(8,128)(2,1)S(1)} %copy-done.4, bf16[7,80,256]{2,1,0:T(8,128)(2,1)S(1)} %collective-permute-done.2.up, bf16[6,80,256]{2,1,0:T(8,128)(2,1)S(1)} %collective-permute-done.3.down, ...), custom_call_target="tpu_custom_call" | custom-call | flops 6000000000 | bytes 4194304 | tf_op jit(solution)/shard_map/pallas_call | solution.py:457
  29.9 24.9 %all_to_all.10 = bf16[64,8,512]{2,1,0:T(8,128)(2,1)S(1)} all-to-all(bf16[64,8,512]{2,1,0:T(8,128)(2,1)S(1)} %bitcast.18), channel_id=1, replica_groups=mesh['gz'=4,'gi'=8,'gx'=8] {'gi','gx'}, dimensions={0} | all-to-all | bytes 1048576 | tf_op jit(solution)/shard_map/all_to_all | solution.py:575
  54.8 1.7 %collective-permute-start.4 = (bf16[128,512]{1,0:T(8,128)(2,1)S(1)}, bf16[128,512]{1,0:T(8,128)(2,1)S(1)}, u32[]{:S(2)}, u32[]{:S(2)}) collective-permute-start(bf16[128,512]{1,0:T(8,128)(2,1)S(1)} %get-tuple-element.38), channel_id=1, source_target_pairs={{0,64},{1,65},{2,66},{3,67},{4,68},{5,69},{6,70},{7,71},{8,72},{9,... | collective-permute-start | bytes 393224 | tf_op jit(solution)/shard_map/ppermute | solution.py:561
  56.4 2.6 %collective-permute-start.5 = (bf16[128,512]{1,0:T(8,128)(2,1)S(1)}, bf16[128,512]{1,0:T(8,128)(2,1)S(1)}, u32[]{:S(2)}, u32[]{:S(2)}) collective-permute-start(bf16[128,512]{1,0:T(8,128)(2,1)S(1)} %get-tuple-element.37), channel_id=1, source_target_pairs={{0,192},{1,193},{2,194},{3,195},{4,196},{5,197},{6,198},{7,199},{8... | collective-permute-start | bytes 393224 | tf_op jit(solution)/shard_map/ppermute | solution.py:561
  59.0 1.2 %copy-done.18 = f32[2,512,256]{2,1,0:T(8,128)S(1)} copy-done((f32[2,512,256]{2,1,0:T(8,128)S(1)}, f32[2,512,256]{2,1,0:T(8,128)}, u32[]{:S(2)}) %copy-start.18) | copy-done | bytes 1048600
  60.3 4.1 %shard_map.265 = (bf16[448,512]{1,0:T(8,128)(2,1)S(1)}, bf16[448,512]{1,0:T(8,128)(2,1)S(1)}, bf16[256,512]{1,0:T(8,128)(2,1)S(1)}, bf16[128,512]{1,0:T(8,128)(2,1)S(1)}, bf16[256,512]{1,0:T(8,128)(2,1)S(1)}) custom-call(s32[6]{0:T(128)S(1)} %stack.15.pos, bf16[2,512,1536]{2,1,0:T(8,128)(2,1)S(1)} %copy-done.2, bf16[2,512,512]{2,1,0:T(8,128)(2,1)S(1)} %copy-done.4, ...), custom_call_target="tpu_custom_call" | custom-call | flops 6000000000 | bytes 4194304 | tf_op jit(solution)/shard_map/pallas_call | solution.py:457
  64.4 0.8 collective-permute-done.4.above
  65.1 0.3 collective-permute-done.5.below
  65.4 3.5 %shard_map.266 = bf16[512,512]{1,0:T(8,128)(2,1)S(1)} custom-call(s32[6]{0:T(128)S(1)} %stack.15.pos, bf16[2,512,1536]{2,1,0:T(8,128)(2,1)S(1)} %copy-done.2, bf16[2,512,512]{2,1,0:T(8,128)(2,1)S(1)} %copy-done.4, bf16[128,512]{1,0:T(8,128)(2,1)S(1)} %collective-permute-done.4.above, bf16[128,512]{1,0:T(8,128)(2,1)S(1)} %collective-permute-done.5.below, ...), custom_call_target="tpu_custom_call" | custom-call | flops 4000000000 | bytes 4194304 | tf_op jit(solution)/shard_map/pallas_call | solution.py:457
  68.9 16.5 %all_to_all.11 = bf16[64,8,512]{2,1,0:T(8,128)(2,1)S(1)} all-to-all(bf16[64,8,512]{2,1,0:T(8,128)(2,1)S(1)} %bitcast.19), channel_id=1, replica_groups=mesh['gz'=4,'gi'=8,'gx'=8] {'gi','gx'}, dimensions={0} | all-to-all | bytes 1048576 | tf_op jit(solution)/shard_map/all_to_all | solution.py:580
  85.4 1.1 %shard_map.267 = bf16[16,32,512]{2,1,0:T(8,128)(2,1)} custom-call(bf16[512,512]{1,0:T(8,128)(2,1)S(1)} %bitcast.15, bf16[64,64]{1,0:T(8,128)(2,1)S(1)} %copy-done.1), custom_call_target="tpu_custom_call" | custom-call | flops 100000000 | bytes 4194304 | tf_op jit(solution)/shard_map/pallas_call | solution.py:457
  (41 shorter events, 0.1 us)
Async XLA Ops:
  1.0 9.5 %collective-permute-start = (bf16[32,8,256]{2,1,0:T(8,128)(2,1)S(1)}, bf16[32,8,256]{2,1,0:T(8,128)(2,1)S(1)}, u32[]{:S(2)}, u32[]{:S(2)}) collective-permute-start(bf16[32,8,256]{2,1,0:T(8,128)(2,1)S(1)} %get-tuple-element.35), channel_id=1, source_target_pairs={{0,1},{1,2},{2,3},{3,4},{4,5},{5,6},{6,7},{7,0},{8,9},{9,10},{10,1... | collective-permute-start | bytes 393224 | tf_op jit(solution)/shard_map/ppermute | solution.py:561
  3.5 7.0 %slice-start = ((bf16[32,64,256]{2,1,0:T(8,128)(2,1)}), bf16[6,64,256]{2,1,0:T(8,128)(2,1)S(1)}, s32[]{:S(2)}) async-start(bf16[32,64,256]{2,1,0:T(8,128)(2,1)} %own_hbm.3), calls=%async_computation.2 | async-start | bytes 393216 | tf_op jit(solution)/shard_map/slice | solution.py:570
  3.5 9.8 %slice-start.1 = ((bf16[32,64,256]{2,1,0:T(8,128)(2,1)}), bf16[7,64,256]{2,1,0:T(8,128)(2,1)S(1)}, s32[]{:S(2)}) async-start(bf16[32,64,256]{2,1,0:T(8,128)(2,1)} %own_hbm.3), calls=%async_computation.3 | async-start | bytes 458752 | tf_op jit(solution)/shard_map/slice | solution.py:570
  3.5 10.1 %copy-start = (bf16[32,64,256]{2,1,0:T(8,128)(2,1)S(1)}, bf16[32,64,256]{2,1,0:T(8,128)(2,1)}, u32[]{:S(2)}) copy-start(bf16[32,64,256]{2,1,0:T(8,128)(2,1)} %own_hbm.3) | copy-start | bytes 3145732
  3.5 10.1 %copy-start.4 = (bf16[2,512,512]{2,1,0:T(8,128)(2,1)S(1)}, bf16[2,512,512]{2,1,0:T(8,128)(2,1)}, u32[]{:S(2)}) copy-start(bf16[2,512,512]{2,1,0:T(8,128)(2,1)} %wout_hbm.7) | copy-start | bytes 3145732
  3.5 10.1 %copy-start.5 = (f32[2,1536]{1,0:T(2,128)S(1)}, f32[2,1536]{1,0:T(2,128)}, u32[]{:S(2)}) copy-start(f32[2,1536]{1,0:T(2,128)} %bqkv.7) | copy-start | bytes 36868
  3.6 10.1 %copy-start.6 = (f32[2,512]{1,0:T(2,128)S(1)}, f32[2,512]{1,0:T(2,128)}, u32[]{:S(2)}) copy-start(f32[2,512]{1,0:T(2,128)} %gains.7) | copy-start | bytes 12292
  3.6 10.1 %copy-start.7 = (f32[2,512]{1,0:T(2,128)S(1)}, f32[2,512]{1,0:T(2,128)}, u32[]{:S(2)}) copy-start(f32[2,512]{1,0:T(2,128)} %shifts.7) | copy-start | bytes 12292
  3.6 10.1 %copy-start.8 = (f32[2,512]{1,0:T(2,128)S(1)}, f32[2,512]{1,0:T(2,128)}, u32[]{:S(2)}) copy-start(f32[2,512]{1,0:T(2,128)} %bout.7) | copy-start | bytes 12292
  3.6 10.1 %copy-start.9 = (f32[512]{0:T(512)S(1)}, f32[512]{0:T(512)}, u32[]{:S(2)}) copy-start(f32[512]{0:T(512)} %param.30) | copy-start | bytes 6148
  3.6 10.1 %copy-start.10 = (f32[512]{0:T(512)S(1)}, f32[512]{0:T(512)}, u32[]{:S(2)}) copy-start(f32[512]{0:T(512)} %param.31) | copy-start | bytes 6148
  3.6 10.1 %copy-start.11 = (f32[512]{0:T(512)S(1)}, f32[512]{0:T(512)}, u32[]{:S(2)}) copy-start(f32[512]{0:T(512)} %param.32) | copy-start | bytes 6148
  3.6 10.1 %copy-start.13 = (bf16[240,160]{1,0:T(8,128)(2,1)S(1)}, bf16[240,160]{1,0:T(8,128)(2,1)}, u32[]{:S(2)}) copy-start(bf16[240,160]{1,0:T(8,128)(2,1)} %constant.46.clone.pick) | copy-start | bytes 230404
  3.6 10.1 %copy-start.14 = (bf16[2,64,256]{2,1,0:T(8,128)(2,1)S(1)}, bf16[2,64,256]{2,1,0:T(8,128)(2,1)}, u32[]{:S(2)}) copy-start(bf16[2,64,256]{2,1,0:T(8,128)(2,1)} %constant.49.clone.qsel) | copy-start | bytes 196612
  3.7 10.1 %copy-start.16 = (s32[8,256]{1,0:T(8,128)S(1)}, s32[8,256]{1,0:T(8,128)}, u32[]{:S(2)}) copy-start(s32[8,256]{1,0:T(8,128)} %constant.47.clone.krow) | copy-start | bytes 24580
  3.7 10.1 %copy-start.17 = (s32[8,256]{1,0:T(8,128)S(1)}, s32[8,256]{1,0:T(8,128)}, u32[]{:S(2)}) copy-start(s32[8,256]{1,0:T(8,128)} %constant.48.clone.kcol) | copy-start | bytes 24580
  3.7 6.8 %collective-permute-start.1 = (bf16[32,8,256]{2,1,0:T(8,128)(2,1)S(1)}, bf16[32,8,256]{2,1,0:T(8,128)(2,1)S(1)}, u32[]{:S(2)}, u32[]{:S(2)}) collective-permute-start(bf16[32,8,256]{2,1,0:T(8,128)(2,1)S(1)} %get-tuple-element.36), channel_id=1, source_target_pairs={{0,7},{1,0},{2,1},{3,2},{4,3},{5,4},{6,5},{7,6},{8,15},{9,8},{10,9... | collective-permute-start | bytes 393224 | tf_op jit(solution)/shard_map/ppermute | solution.py:561
  10.5 13.7 %collective-permute-start.3 = (bf16[6,80,256]{2,1,0:T(8,128)(2,1)S(1)}, bf16[6,80,256]{2,1,0:T(8,128)(2,1)S(1)}, u32[]{:S(2)}, u32[]{:S(2)}) collective-permute-start(bf16[6,80,256]{2,1,0:T(8,128)(2,1)S(1)} %pad_maximum_fusion.1), channel_id=1, source_target_pairs={{0,248},{1,249},{2,250},{3,251},{4,252},{5,253},{6,254},{7,255},{8... | collective-permute-start | bytes 737288 | tf_op jit(solution)/shard_map/ppermute | solution.py:561
  13.3 10.9 %collective-permute-start.2 = (bf16[7,80,256]{2,1,0:T(8,128)(2,1)S(1)}, bf16[7,80,256]{2,1,0:T(8,128)(2,1)S(1)}, u32[]{:S(2)}, u32[]{:S(2)}) collective-permute-start(bf16[7,80,256]{2,1,0:T(8,128)(2,1)S(1)} %pad_maximum_fusion), channel_id=1, source_target_pairs={{0,8},{1,9},{2,10},{3,11},{4,12},{5,13},{6,14},{7,15},{8,16},{9,17... | collective-permute-start | bytes 860168 | tf_op jit(solution)/shard_map/ppermute | solution.py:561
  13.7 1.7 %copy-start.3 = (bf16[3,3,256,512]{3,2,1,0:T(8,128)(2,1)S(1)}, bf16[3,3,256,512]{3,2,1,0:T(8,128)(2,1)}, u32[]{:S(2)}) copy-start(bf16[3,3,256,512]{3,2,1,0:T(8,128)(2,1)} %param.29) | copy-start | bytes 7077892
  15.4 1.6 %copy-start.19 = (f32[2,2,512,256]{3,2,1,0:T(8,128)S(1)}, f32[2,2,512,256]{3,2,1,0:T(8,128)}, u32[]{:S(2)}) copy-start(f32[2,2,512,256]{3,2,1,0:T(8,128)} %get-tuple-element.20.table_hbm) | copy-start | bytes 6291460
  17.0 7.2 %copy-start.12 = (bf16[2,256,256]{2,1,0:T(8,128)(2,1)S(1)}, bf16[2,256,256]{2,1,0:T(8,128)(2,1)}, u32[]{:S(2)}) copy-start(bf16[2,256,256]{2,1,0:T(8,128)(2,1)} %constant.50.clone.send) | copy-start | bytes 786436
  24.2 34.8 %copy-start.2 = (bf16[2,512,1536]{2,1,0:T(8,128)(2,1)S(1)}, bf16[2,512,1536]{2,1,0:T(8,128)(2,1)}, u32[]{:S(2)}) copy-start(bf16[2,512,1536]{2,1,0:T(8,128)(2,1)} %wqkv_hbm.5) | copy-start | bytes 9437188
  24.3 34.8 %copy-start.15 = (bf16[64,128]{1,0:T(8,128)(2,1)S(1)}, bf16[64,128]{1,0:T(8,128)(2,1)}, u32[]{:S(2)}) copy-start(bf16[64,128]{1,0:T(8,128)(2,1)} %constant.51.clone.ksel) | copy-start | bytes 49156
  54.8 10.4 %collective-permute-start.4 = (bf16[128,512]{1,0:T(8,128)(2,1)S(1)}, bf16[128,512]{1,0:T(8,128)(2,1)S(1)}, u32[]{:S(2)}, u32[]{:S(2)}) collective-permute-start(bf16[128,512]{1,0:T(8,128)(2,1)S(1)} %get-tuple-element.38), channel_id=1, source_target_pairs={{0,64},{1,65},{2,66},{3,67},{4,68},{5,69},{6,70},{7,71},{8,72},{9,... | collective-permute-start | bytes 393224 | tf_op jit(solution)/shard_map/ppermute | solution.py:561
  56.4 9.0 %collective-permute-start.5 = (bf16[128,512]{1,0:T(8,128)(2,1)S(1)}, bf16[128,512]{1,0:T(8,128)(2,1)S(1)}, u32[]{:S(2)}, u32[]{:S(2)}) collective-permute-start(bf16[128,512]{1,0:T(8,128)(2,1)S(1)} %get-tuple-element.37), channel_id=1, source_target_pairs={{0,192},{1,193},{2,194},{3,195},{4,196},{5,197},{6,198},{7,199},{8... | collective-permute-start | bytes 393224 | tf_op jit(solution)/shard_map/ppermute | solution.py:561
  59.0 1.2 %copy-start.18 = (f32[2,512,256]{2,1,0:T(8,128)S(1)}, f32[2,512,256]{2,1,0:T(8,128)}, u32[]{:S(2)}) copy-start(f32[2,512,256]{2,1,0:T(8,128)} %get-tuple-element.29.table) | copy-start | bytes 3145732
  65.4 20.0 %copy-start.1 = (bf16[64,64]{1,0:T(8,128)(2,1)S(1)}, bf16[64,64]{1,0:T(8,128)(2,1)}, u32[]{:S(2)}) copy-start(bf16[64,64]{1,0:T(8,128)(2,1)} %constant.52.clone.sel) | copy-start | bytes 24580

commit v4 on v3

--- a/solution.py
+++ b/solution.py
@@ -24,7 +24,7 @@
 PT = 80
 NTOK = PAIRS * PT
 EPS = 1e-5
-VMEM_TABLE, VMEM_NEAR, VMEM_FAR, VMEM_BACK = 56, 39, 46, 46
+VMEM_TABLE, VMEM_NEAR, VMEM_FAR, VMEM_BACK = 56, 40, 46, 46
 
 
 def pair_slots():

time: 86.8 us -> 88.5 us (1.020)
  waiting for transfers between devices: 1.05 us -> 2.27 us
    ppermute x6, waiting for transfers between devices: 1.05 us -> 2.27 us  [shifted(): return lax.ppermute(x, ('gz', 'gi', 'gx'), pairs)]
    unnamed x40 -> x42, local copies, waits for them, and re-layouts: 4.58 us -> 4.6 us
where the time goes in v4:
time: 88.5 us; the launch traced here: 88.2 us
  blocking collectives  41.3 us (47%)
  Pallas kernels  26.3 us (30%)
  starting transfers between devices  12.2 us (14%)
  local copies, waits for them, and re-layouts  5.71 us (6%)
  waiting for transfers between devices  2.27 us (3%)
    pallas_call x6, Pallas kernels, call(): pl.pallas_call(kernel, out_shape=[jax.ShapeDtypeStruct(s, t) for s, t in...  26.3 us
    all_to_all x1, blocking collectives, per_device(): lax.all_to_all(x1.reshape(64, 8, C3), ('gi', 'gx'), 0, 0).reshape(512, C3)  24.8 us
    all_to_all x1, blocking collectives, per_device(): lax.all_to_all(x2.reshape(64, 8, C3), ('gi', 'gx'), 0, 0).reshape(512, C3)  16.5 us
    ppermute x6, starting transfers between devices, shifted(): return lax.ppermute(x, ('gz', 'gi', 'gx'), pairs)  12.2 us
    unnamed x42, local copies, waits for them, and re-layouts  4.6 us
    ppermute x6, waiting for transfers between devices, shifted(): return lax.ppermute(x, ('gz', 'gi', 'gx'), pairs)  2.27 us
  transfers between devices with their start and end apart: 6, of which 2 were waited for; matrix products, arithmetic and copies ran while one was open for 0% of the time, Pallas kernels for 18%

profile of v4, /device:TPU:1, one launch (start us, length us, event | category | flops | bytes accessed | tf_op | source)
XLA Modules:
  0.0 88.2 jit_solution(8083599664115338790)
XLA Ops:
  0.0 1.0 %fusion = (bf16[32,8,256]{2,1,0:T(8,128)(2,1)S(1)}, bf16[32,8,256]{2,1,0:T(8,128)(2,1)S(1)}) fusion(bf16[32,64,256]{2,1,0:T(8,128)(2,1)} %own_hbm.3), kind=kLoop, calls=%fused_computation.4 | loop fusion | bytes 524288 | tf_op jit(solution)/shard_map/slice | solution.py:564
  1.0 2.5 %collective-permute-start = (bf16[32,8,256]{2,1,0:T(8,128)(2,1)S(1)}, bf16[32,8,256]{2,1,0:T(8,128)(2,1)S(1)}, u32[]{:S(2)}, u32[]{:S(2)}) collective-permute-start(bf16[32,8,256]{2,1,0:T(8,128)(2,1)S(1)} %get-tuple-element.35), channel_id=1, source_target_pairs={{0,1},{1,2},{2,3},{3,4},{4,5},{5,6},{6,7},{7,0},{8,9},{9,10},{10,1... | collective-permute-start | bytes 393224 | tf_op jit(solution)/shard_map/ppermute | solution.py:561
  3.5 0.0 copy-start.4
  3.6 0.0 copy-start.5
  3.6 0.0 copy-start.6
  3.6 0.0 copy-start.7
  3.6 0.0 copy-start.8
  3.6 0.0 copy-start.9
  3.6 0.0 copy-start.10
  3.6 0.0 copy-start.12
  3.6 0.0 copy-start.13
  3.7 0.0 copy-start.15
  3.7 0.0 copy-start.16
  3.7 2.3 %collective-permute-start.1 = (bf16[32,8,256]{2,1,0:T(8,128)(2,1)S(1)}, bf16[32,8,256]{2,1,0:T(8,128)(2,1)S(1)}, u32[]{:S(2)}, u32[]{:S(2)}) collective-permute-start(bf16[32,8,256]{2,1,0:T(8,128)(2,1)S(1)} %get-tuple-element.36), channel_id=1, source_target_pairs={{0,7},{1,0},{2,1},{3,2},{4,3},{5,4},{6,5},{7,6},{8,15},{9,8},{10,9... | collective-permute-start | bytes 393224 | tf_op jit(solution)/shard_map/ppermute | solution.py:561
  6.0 4.4 %shard_map.262 = (f32[2,2,512,256]{3,2,1,0:T(8,128)}, f32[2,512,256]{2,1,0:T(8,128)}) custom-call(f32[2,16,49]{2,1,0:T(8,128)} %rel.1, bf16[49,4096]{1,0:T(8,128)(2,1)} %constant.42.clone.hot0, s32[2,64,256]{2,1,0:T(8,128)} %constant.43.clone.code0, bf16[49,512]{1,0:T(8,128)(2,1)} %constant.44.clone.hot1, s32[64,256]{1,0:T(8,128)} %constant.45.clone.code1), custom_call_target="tpu_custom_call" | custom-call | flops 3000000000 | bytes 4194304 | tf_op jit(solution)/shard_map/pallas_call | solution.py:457
  10.4 0.1 stack.15.pos
  10.5 2.7 %collective-permute-start.3 = (bf16[6,80,256]{2,1,0:T(8,128)(2,1)S(1)}, bf16[6,80,256]{2,1,0:T(8,128)(2,1)S(1)}, u32[]{:S(2)}, u32[]{:S(2)}) collective-permute-start(bf16[6,80,256]{2,1,0:T(8,128)(2,1)S(1)} %pad_maximum_fusion.1), channel_id=1, source_target_pairs={{0,248},{1,249},{2,250},{3,251},{4,252},{5,253},{6,254},{7,255},{8... | collective-permute-start | bytes 737288 | tf_op jit(solution)/shard_map/ppermute | solution.py:561
  13.3 0.3 collective-permute-start.2
  13.7 1.6 %copy-done.20 = f32[2,2,512,256]{3,2,1,0:T(8,128)S(1)} copy-done((f32[2,2,512,256]{3,2,1,0:T(8,128)S(1)}, f32[2,2,512,256]{3,2,1,0:T(8,128)}, u32[]{:S(2)}) %copy-start.20) | copy-done | bytes 2097176
  15.3 7.7 %shard_map.263 = (bf16[7,80,512]{2,1,0:T(8,128)(2,1)S(1)}, bf16[7,80,512]{2,1,0:T(8,128)(2,1)S(1)}, bf16[7,80,512]{2,1,0:T(8,128)(2,1)S(1)}, bf16[7,80,512]{2,1,...) custom-call(s32[6]{0:T(128)S(1)} %stack.15.pos, ...), custom_call_target="tpu_custom_call" | custom-call | flops 8000000000 | bytes 4194304 | tf_op jit(solution)/shard_map/pallas_call | solution.py:457
  23.0 1.3 %copy-done.18 = f32[2,2,512,256]{3,2,1,0:T(8,128)} copy-done((f32[2,2,512,256]{3,2,1,0:T(8,128)}, f32[2,2,512,256]{3,2,1,0:T(8,128)S(1)}, u32[]{:S(2)}) %copy-start.18) | copy-done | bytes 2097176
  24.4 1.6 %copy-done.19 = f32[2,2,512,256]{3,2,1,0:T(8,128)S(1)} copy-done((f32[2,2,512,256]{3,2,1,0:T(8,128)S(1)}, f32[2,2,512,256]{3,2,1,0:T(8,128)}, u32[]{:S(2)}) %copy-start.19) | copy-done | bytes 2097176
  26.0 5.6 %shard_map.264 = bf16[512,512]{1,0:T(8,128)(2,1)S(1)} custom-call(s32[6]{0:T(128)S(1)} %stack.15.pos, bf16[32,64,256]{2,1,0:T(8,128)(2,1)S(1)} %copy-done, bf16[2,512,512]{2,1,0:T(8,128)(2,1)S(1)} %copy-done.3, bf16[7,80,256]{2,1,0:T(8,128)(2,1)S(1)} %collective-permute-done.2.up, bf16[6,80,256]{2,1,0:T(8,128)(2,1)S(1)} %collective-permute-done.3.down, ...), custom_call_target="tpu_custom_call" | custom-call | flops 6000000000 | bytes 4194304 | tf_op jit(solution)/shard_map/pallas_call | solution.py:457
  31.5 24.8 %all_to_all.10 = bf16[64,8,512]{2,1,0:T(8,128)(2,1)S(1)} all-to-all(bf16[64,8,512]{2,1,0:T(8,128)(2,1)S(1)} %bitcast.18), channel_id=1, replica_groups=mesh['gz'=4,'gi'=8,'gx'=8] {'gi','gx'}, dimensions={0} | all-to-all | bytes 1048576 | tf_op jit(solution)/shard_map/all_to_all | solution.py:575
  56.4 1.8 %collective-permute-start.4 = (bf16[128,512]{1,0:T(8,128)(2,1)S(1)}, bf16[128,512]{1,0:T(8,128)(2,1)S(1)}, u32[]{:S(2)}, u32[]{:S(2)}) collective-permute-start(bf16[128,512]{1,0:T(8,128)(2,1)S(1)} %get-tuple-element.38), channel_id=1, source_target_pairs={{0,64},{1,65},{2,66},{3,67},{4,68},{5,69},{6,70},{7,71},{8,72},{9,... | collective-permute-start | bytes 393224 | tf_op jit(solution)/shard_map/ppermute | solution.py:561
  58.1 2.6 %collective-permute-start.5 = (bf16[128,512]{1,0:T(8,128)(2,1)S(1)}, bf16[128,512]{1,0:T(8,128)(2,1)S(1)}, u32[]{:S(2)}, u32[]{:S(2)}) collective-permute-start(bf16[128,512]{1,0:T(8,128)(2,1)S(1)} %get-tuple-element.37), channel_id=1, source_target_pairs={{0,192},{1,193},{2,194},{3,195},{4,196},{5,197},{6,198},{7,199},{8... | collective-permute-start | bytes 393224 | tf_op jit(solution)/shard_map/ppermute | solution.py:561
  60.7 4.1 %shard_map.265 = (bf16[448,512]{1,0:T(8,128)(2,1)S(1)}, bf16[448,512]{1,0:T(8,128)(2,1)S(1)}, bf16[256,512]{1,0:T(8,128)(2,1)S(1)}, bf16[128,512]{1,0:T(8,128)(2,1)S(1)}, bf16[256,512]{1,0:T(8,128)(2,1)S(1)}) custom-call(s32[6]{0:T(128)S(1)} %stack.15.pos, bf16[2,512,1536]{2,1,0:T(8,128)(2,1)S(1)} %copy-done.2, bf16[2,512,512]{2,1,0:T(8,128)(2,1)S(1)} %copy-done.3, ...), custom_call_target="tpu_custom_call" | custom-call | flops 6000000000 | bytes 4194304 | tf_op jit(solution)/shard_map/pallas_call | solution.py:457
  64.8 2.0 %collective-permute-done.4.above = bf16[128,512]{1,0:T(8,128)(2,1)S(1)} collective-permute-done((bf16[128,512]{1,0:T(8,128)(2,1)S(1)}, bf16[128,512]{1,0:T(8,128)(2,1)S(1)}, u32[]{:S(2)}, u32[]{:S(2)}) %collective-permute-start.4) | collective-permute-done | bytes 131104 | tf_op jit(solution)/shard_map/ppermute | solution.py:561
  66.8 0.3 collective-permute-done.5.below
  67.1 3.5 %shard_map.266 = bf16[512,512]{1,0:T(8,128)(2,1)S(1)} custom-call(s32[6]{0:T(128)S(1)} %stack.15.pos, bf16[2,512,1536]{2,1,0:T(8,128)(2,1)S(1)} %copy-done.2, bf16[2,512,512]{2,1,0:T(8,128)(2,1)S(1)} %copy-done.3, bf16[128,512]{1,0:T(8,128)(2,1)S(1)} %collective-permute-done.4.above, bf16[128,512]{1,0:T(8,128)(2,1)S(1)} %collective-permute-done.5.below, ...), custom_call_target="tpu_custom_call" | custom-call | flops 4000000000 | bytes 4194304 | tf_op jit(solution)/shard_map/pallas_call | solution.py:457
  70.6 16.5 %all_to_all.11 = bf16[64,8,512]{2,1,0:T(8,128)(2,1)S(1)} all-to-all(bf16[64,8,512]{2,1,0:T(8,128)(2,1)S(1)} %bitcast.19), channel_id=1, replica_groups=mesh['gz'=4,'gi'=8,'gx'=8] {'gi','gx'}, dimensions={0} | all-to-all | bytes 1048576 | tf_op jit(solution)/shard_map/all_to_all | solution.py:580
  87.1 1.1 %shard_map.267 = bf16[16,32,512]{2,1,0:T(8,128)(2,1)} custom-call(bf16[512,512]{1,0:T(8,128)(2,1)S(1)} %bitcast.15, bf16[64,64]{1,0:T(8,128)(2,1)S(1)} %copy-done.1), custom_call_target="tpu_custom_call" | custom-call | flops 100000000 | bytes 4194304 | tf_op jit(solution)/shard_map/pallas_call | solution.py:457
  (43 shorter events, 0.1 us)
Async XLA Ops:
  1.0 9.5 %collective-permute-start = (bf16[32,8,256]{2,1,0:T(8,128)(2,1)S(1)}, bf16[32,8,256]{2,1,0:T(8,128)(2,1)S(1)}, u32[]{:S(2)}, u32[]{:S(2)}) collective-permute-start(bf16[32,8,256]{2,1,0:T(8,128)(2,1)S(1)} %get-tuple-element.35), channel_id=1, source_target_pairs={{0,1},{1,2},{2,3},{3,4},{4,5},{5,6},{6,7},{7,0},{8,9},{9,10},{10,1... | collective-permute-start | bytes 393224 | tf_op jit(solution)/shard_map/ppermute | solution.py:561
  3.5 7.0 %slice-start = ((bf16[32,64,256]{2,1,0:T(8,128)(2,1)}), bf16[6,64,256]{2,1,0:T(8,128)(2,1)S(1)}, s32[]{:S(2)}) async-start(bf16[32,64,256]{2,1,0:T(8,128)(2,1)} %own_hbm.3), calls=%async_computation.2 | async-start | bytes 393216 | tf_op jit(solution)/shard_map/slice | solution.py:570
  3.5 9.8 %slice-start.1 = ((bf16[32,64,256]{2,1,0:T(8,128)(2,1)}), bf16[7,64,256]{2,1,0:T(8,128)(2,1)S(1)}, s32[]{:S(2)}) async-start(bf16[32,64,256]{2,1,0:T(8,128)(2,1)} %own_hbm.3), calls=%async_computation.3 | async-start | bytes 458752 | tf_op jit(solution)/shard_map/slice | solution.py:570
  3.5 10.1 %copy-start = (bf16[32,64,256]{2,1,0:T(8,128)(2,1)S(1)}, bf16[32,64,256]{2,1,0:T(8,128)(2,1)}, u32[]{:S(2)}) copy-start(bf16[32,64,256]{2,1,0:T(8,128)(2,1)} %own_hbm.3) | copy-start | bytes 3145732
  3.5 10.1 %copy-start.3 = (bf16[2,512,512]{2,1,0:T(8,128)(2,1)S(1)}, bf16[2,512,512]{2,1,0:T(8,128)(2,1)}, u32[]{:S(2)}) copy-start(bf16[2,512,512]{2,1,0:T(8,128)(2,1)} %wout_hbm.7) | copy-start | bytes 3145732
  3.5 10.1 %copy-start.4 = (f32[2,1536]{1,0:T(2,128)S(1)}, f32[2,1536]{1,0:T(2,128)}, u32[]{:S(2)}) copy-start(f32[2,1536]{1,0:T(2,128)} %bqkv.7) | copy-start | bytes 36868
  3.6 10.1 %copy-start.5 = (f32[2,512]{1,0:T(2,128)S(1)}, f32[2,512]{1,0:T(2,128)}, u32[]{:S(2)}) copy-start(f32[2,512]{1,0:T(2,128)} %gains.7) | copy-start | bytes 12292
  3.6 10.1 %copy-start.6 = (f32[2,512]{1,0:T(2,128)S(1)}, f32[2,512]{1,0:T(2,128)}, u32[]{:S(2)}) copy-start(f32[2,512]{1,0:T(2,128)} %shifts.7) | copy-start | bytes 12292
  3.6 10.1 %copy-start.7 = (f32[2,512]{1,0:T(2,128)S(1)}, f32[2,512]{1,0:T(2,128)}, u32[]{:S(2)}) copy-start(f32[2,512]{1,0:T(2,128)} %bout.7) | copy-start | bytes 12292
  3.6 10.1 %copy-start.8 = (f32[512]{0:T(512)S(1)}, f32[512]{0:T(512)}, u32[]{:S(2)}) copy-start(f32[512]{0:T(512)} %param.30) | copy-start | bytes 6148
  3.6 10.1 %copy-start.9 = (f32[512]{0:T(512)S(1)}, f32[512]{0:T(512)}, u32[]{:S(2)}) copy-start(f32[512]{0:T(512)} %param.31) | copy-start | bytes 6148
  3.6 10.1 %copy-start.10 = (f32[512]{0:T(512)S(1)}, f32[512]{0:T(512)}, u32[]{:S(2)}) copy-start(f32[512]{0:T(512)} %param.32) | copy-start | bytes 6148
  3.6 10.1 %copy-start.12 = (bf16[240,160]{1,0:T(8,128)(2,1)S(1)}, bf16[240,160]{1,0:T(8,128)(2,1)}, u32[]{:S(2)}) copy-start(bf16[240,160]{1,0:T(8,128)(2,1)} %constant.46.clone.pick) | copy-start | bytes 230404
  3.6 10.1 %copy-start.13 = (bf16[2,64,256]{2,1,0:T(8,128)(2,1)S(1)}, bf16[2,64,256]{2,1,0:T(8,128)(2,1)}, u32[]{:S(2)}) copy-start(bf16[2,64,256]{2,1,0:T(8,128)(2,1)} %constant.49.clone.qsel) | copy-start | bytes 196612
  3.7 10.1 %copy-start.15 = (s32[8,256]{1,0:T(8,128)S(1)}, s32[8,256]{1,0:T(8,128)}, u32[]{:S(2)}) copy-start(s32[8,256]{1,0:T(8,128)} %constant.47.clone.krow) | copy-start | bytes 24580
  3.7 10.1 %copy-start.16 = (s32[8,256]{1,0:T(8,128)S(1)}, s32[8,256]{1,0:T(8,128)}, u32[]{:S(2)}) copy-start(s32[8,256]{1,0:T(8,128)} %constant.48.clone.kcol) | copy-start | bytes 24580
  3.7 6.8 %collective-permute-start.1 = (bf16[32,8,256]{2,1,0:T(8,128)(2,1)S(1)}, bf16[32,8,256]{2,1,0:T(8,128)(2,1)S(1)}, u32[]{:S(2)}, u32[]{:S(2)}) collective-permute-start(bf16[32,8,256]{2,1,0:T(8,128)(2,1)S(1)} %get-tuple-element.36), channel_id=1, source_target_pairs={{0,7},{1,0},{2,1},{3,2},{4,3},{5,4},{6,5},{7,6},{8,15},{9,8},{10,9... | collective-permute-start | bytes 393224 | tf_op jit(solution)/shard_map/ppermute | solution.py:561
  10.5 13.8 %collective-permute-start.3 = (bf16[6,80,256]{2,1,0:T(8,128)(2,1)S(1)}, bf16[6,80,256]{2,1,0:T(8,128)(2,1)S(1)}, u32[]{:S(2)}, u32[]{:S(2)}) collective-permute-start(bf16[6,80,256]{2,1,0:T(8,128)(2,1)S(1)} %pad_maximum_fusion.1), channel_id=1, source_target_pairs={{0,248},{1,249},{2,250},{3,251},{4,252},{5,253},{6,254},{7,255},{8... | collective-permute-start | bytes 737288 | tf_op jit(solution)/shard_map/ppermute | solution.py:561
  13.3 11.0 %collective-permute-start.2 = (bf16[7,80,256]{2,1,0:T(8,128)(2,1)S(1)}, bf16[7,80,256]{2,1,0:T(8,128)(2,1)S(1)}, u32[]{:S(2)}, u32[]{:S(2)}) collective-permute-start(bf16[7,80,256]{2,1,0:T(8,128)(2,1)S(1)} %pad_maximum_fusion), channel_id=1, source_target_pairs={{0,8},{1,9},{2,10},{3,11},{4,12},{5,13},{6,14},{7,15},{8,16},{9,17... | collective-permute-start | bytes 860168 | tf_op jit(solution)/shard_map/ppermute | solution.py:561
  13.7 1.6 %copy-start.20 = (f32[2,2,512,256]{3,2,1,0:T(8,128)S(1)}, f32[2,2,512,256]{3,2,1,0:T(8,128)}, u32[]{:S(2)}) copy-start(f32[2,2,512,256]{3,2,1,0:T(8,128)} %get-tuple-element.20.table_hbm) | copy-start | bytes 6291460
  15.3 9.0 %copy-start.11 = (bf16[2,256,256]{2,1,0:T(8,128)(2,1)S(1)}, bf16[2,256,256]{2,1,0:T(8,128)(2,1)}, u32[]{:S(2)}) copy-start(bf16[2,256,256]{2,1,0:T(8,128)(2,1)} %constant.50.clone.send) | copy-start | bytes 786436
  23.0 1.3 %copy-start.18 = (f32[2,2,512,256]{3,2,1,0:T(8,128)}, f32[2,2,512,256]{3,2,1,0:T(8,128)S(1)}, u32[]{:S(2)}) copy-start(f32[2,2,512,256]{3,2,1,0:T(8,128)S(1)} %get-tuple-element.28.table) | copy-start | bytes 6291460
  24.4 1.6 %copy-start.19 = (f32[2,2,512,256]{3,2,1,0:T(8,128)S(1)}, f32[2,2,512,256]{3,2,1,0:T(8,128)}, u32[]{:S(2)}) copy-start(f32[2,2,512,256]{3,2,1,0:T(8,128)} %copy-done.18) | copy-start | bytes 6291460
  26.0 34.8 %copy-start.2 = (bf16[2,512,1536]{2,1,0:T(8,128)(2,1)S(1)}, bf16[2,512,1536]{2,1,0:T(8,128)(2,1)}, u32[]{:S(2)}) copy-start(bf16[2,512,1536]{2,1,0:T(8,128)(2,1)} %wqkv_hbm.5) | copy-start | bytes 9437188
  26.0 34.8 %copy-start.14 = (bf16[64,128]{1,0:T(8,128)(2,1)S(1)}, bf16[64,128]{1,0:T(8,128)(2,1)}, u32[]{:S(2)}) copy-start(bf16[64,128]{1,0:T(8,128)(2,1)} %constant.51.clone.ksel) | copy-start | bytes 49156
  26.0 34.8 %copy-start.17 = (f32[2,512,256]{2,1,0:T(8,128)S(1)}, f32[2,512,256]{2,1,0:T(8,128)}, u32[]{:S(2)}) copy-start(f32[2,512,256]{2,1,0:T(8,128)} %get-tuple-element.29.table) | copy-start | bytes 3145732
  56.4 10.5 %collective-permute-start.4 = (bf16[128,512]{1,0:T(8,128)(2,1)S(1)}, bf16[128,512]{1,0:T(8,128)(2,1)S(1)}, u32[]{:S(2)}, u32[]{:S(2)}) collective-permute-start(bf16[128,512]{1,0:T(8,128)(2,1)S(1)} %get-tuple-element.38), channel_id=1, source_target_pairs={{0,64},{1,65},{2,66},{3,67},{4,68},{5,69},{6,70},{7,71},{8,72},{9,... | collective-permute-start | bytes 393224 | tf_op jit(solution)/shard_map/ppermute | solution.py:561
  58.1 9.0 %collective-permute-start.5 = (bf16[128,512]{1,0:T(8,128)(2,1)S(1)}, bf16[128,512]{1,0:T(8,128)(2,1)S(1)}, u32[]{:S(2)}, u32[]{:S(2)}) collective-permute-start(bf16[128,512]{1,0:T(8,128)(2,1)S(1)} %get-tuple-element.37), channel_id=1, source_target_pairs={{0,192},{1,193},{2,194},{3,195},{4,196},{5,197},{6,198},{7,199},{8... | collective-permute-start | bytes 393224 | tf_op jit(solution)/shard_map/ppermute | solution.py:561
  67.1 20.0 %copy-start.1 = (bf16[64,64]{1,0:T(8,128)(2,1)S(1)}, bf16[64,64]{1,0:T(8,128)(2,1)}, u32[]{:S(2)}) copy-start(bf16[64,64]{1,0:T(8,128)(2,1)} %constant.52.clone.sel) | copy-start | bytes 24580
